TPU v7x, 128 devices: a whole 4x4x4 slice. The times are simulated.
128 devices in a mesh: row: 8 (over x, core), col: 16 (over z, y).
Axes of the slice: x: 4, y: 4, z: 4, core: 2. Of those that a mesh axis runs over, the one named last changes fastest.
Arguments:
- features: bfloat16 [2, 16384, 256], P(None, ('row', 'col')), may hold values from -6 to 6
- adjacency: bfloat16 [8, 16, 512, 128, 128], P('row', 'col'), may hold values from -0.09375 to 0.09375
- requests: int32 [8, 16, 16, 2], P('row', 'col'), may hold values from -1 to 15, as said below
- block_coords: int32 [8, 16, 512, 2], P('row', 'col'), may hold values from 0 to 31, as said below
- weight: bfloat16 [256, 256], replicated, may hold values from -0.375 to 0.375
- cotangent: bfloat16 [262144, 256], P(('row', 'col')), may hold values from -6 to 6
Outputs:
- activations: bfloat16 [262144, 256], P(('row', 'col'))
- weight_grad: float32 [256, 256], replicated
- feature_grad: bfloat16 [2, 16384, 256], P(None, ('row', 'col'))
Inputs may be any that keep to these rules, and one draw needn't show every extreme that they name: `requests`: -1 marks an unused entry; a used entry is a block of grid column s counted over the two panels, panel first, then grid row, then block. For each (r, c, s) the used entries come first and are distinct, and each device (r, c) uses all 2 entries for at least one column s. `block_coords`: the first coordinate is an output block of the device. The second is a receive slot s * 2 + j whose entry requests[r, c, s, j] of the same device is used; every used entry is named by at least one nonzero.
All inputs are finite; a program needn't handle non-finite values.
Results may differ from a plain program's by a relative error of at most 0.0063.
Values may be sent and summed in bfloat16 or wider, within the bound.
No kernel may reach another device: no remote copies, remote signals or barrier semaphores. Data moves between devices by JAX's collectives and lax.ppermute only.
A program may use at most 192 MiB of HBM per device.

v0:
```python
import math

import jax
import jax.numpy as jnp
from jax import lax
from jax.sharding import PartitionSpec as P


def select_rows(index, count, table):
    picker = (index[:, None] == jnp.arange(count, dtype=jnp.int32)[None, :]).astype(table.dtype)
    return jnp.dot(picker, table, preferred_element_type=jnp.float32)


def add_rows(index, count, values):
    placer = (index[:, None] == jnp.arange(count, dtype=jnp.int32)[None, :]).astype(jnp.float32)
    return jnp.dot(
        placer.T, values, preferred_element_type=jnp.float32, precision=lax.Precision.HIGHEST
    )


def local(features, adjacency, requests, block_coords, weight, cotangent):
    panels, span, width = features.shape
    block_size = adjacency.shape[-1]
    grid_rows = lax.axis_size("row")
    grid_cols = lax.axis_size("col")
    own_blocks = span // block_size
    out_blocks = cotangent.shape[0] // block_size
    edges = adjacency[0, 0]
    coords = block_coords[0, 0]
    wanted = requests[0, 0]
    per_peer = wanted.shape[1]
    nonzeros = edges.shape[0]
    slot_count = grid_cols * per_peer
    per_group = grid_rows * own_blocks
    group_count = panels * per_group
    flat_size = block_size * width
    out_block = coords[:, 0]
    slot = coords[:, 1]
    incoming = lax.all_to_all(wanted, "col", split_axis=0, concat_axis=0, tiled=True)
    whole = lax.all_gather(features, ("row", "col"), axis=1, tiled=True)
    all_blocks = panels * grid_rows * grid_cols * own_blocks
    flat_whole = whole.reshape(all_blocks, flat_size)
    flat_wanted_own = wanted.reshape(-1)
    source_col = jnp.arange(slot_count, dtype=jnp.int32) // per_peer
    safe_pick = jnp.maximum(flat_wanted_own, 0)
    panel = safe_pick // per_group
    within = safe_pick % per_group
    chooser = (
        panel * (grid_rows * grid_cols * own_blocks)
        + (within // own_blocks * grid_cols + source_col) * own_blocks
        + within % own_blocks
    )
    chooser = jnp.where(flat_wanted_own >= 0, chooser, -1)
    table = select_rows(chooser, all_blocks, flat_whole).astype(jnp.bfloat16)
    step_size = math.gcd(nonzeros, 64)
    steps_count = nonzeros // step_size
    edge_steps = edges.reshape(steps_count, step_size, block_size, block_size)
    row_steps = out_block.reshape(steps_count, step_size)
    slot_steps = slot.reshape(steps_count, step_size)

    def forward_step(total, item):
        edge_part, row_part, slot_part = item
        pieces = (
            select_rows(slot_part, slot_count, table)
            .astype(jnp.bfloat16)
            .reshape(step_size, block_size, width)
        )
        products = jnp.einsum("nij,njf->nif", edge_part, pieces, preferred_element_type=jnp.float32)
        return (
            total + add_rows(row_part, out_blocks, products.reshape(step_size, flat_size)),
            None,
        )

    start = jnp.zeros((out_blocks, flat_size), jnp.float32)
    summed, _ = lax.scan(forward_step, start, (edge_steps, row_steps, slot_steps))
    aggregated = summed.astype(jnp.bfloat16).reshape(out_blocks * block_size, width)
    pre = jnp.dot(aggregated, weight, preferred_element_type=jnp.float32)
    activ, pull = jax.vjp(jax.nn.gelu, pre)
    activations = activ.astype(jnp.bfloat16)
    pre_grad = pull(cotangent.astype(jnp.float32))[0].astype(jnp.bfloat16)
    local_wgrad = jnp.einsum("nf,ng->fg", aggregated, pre_grad, preferred_element_type=jnp.float32)
    weight_grad = lax.psum(local_wgrad, ("row", "col"))
    row_grad = jnp.einsum("ng,fg->nf", pre_grad, weight, preferred_element_type=jnp.float32)
    row_grad = row_grad.astype(jnp.bfloat16).reshape(out_blocks, flat_size)

    def backward_step(total, item):
        edge_part, row_part, slot_part = item
        pieces = (
            select_rows(row_part, out_blocks, row_grad)
            .astype(jnp.bfloat16)
            .reshape(step_size, block_size, width)
        )
        products = jnp.einsum("nji,njf->nif", edge_part, pieces, preferred_element_type=jnp.float32)
        return (
            total + add_rows(slot_part, slot_count, products.reshape(step_size, flat_size)),
            None,
        )

    slot_start = jnp.zeros((slot_count, flat_size), jnp.float32)
    slot_sums, _ = lax.scan(backward_step, slot_start, (edge_steps, row_steps, slot_steps))
    returned = lax.all_to_all(
        slot_sums.reshape(grid_cols, per_peer, block_size, width),
        "col",
        split_axis=0,
        concat_axis=0,
        tiled=True,
    )
    flat_wanted = incoming.reshape(-1)
    group_grad = add_rows(flat_wanted, group_count, returned.reshape(slot_count, flat_size))
    group_grad = group_grad.reshape(panels, grid_rows * span, width)
    owned = lax.psum_scatter(group_grad, "row", scatter_dimension=1, tiled=True)
    return (activations, weight_grad, owned.astype(jnp.bfloat16))


def solution(mesh):
    placed = (
        P(None, ("row", "col"), None),
        P("row", "col", None, None, None),
        P("row", "col", None, None),
        P("row", "col", None, None),
        P(),
        P(("row", "col"), None),
    )
    return jax.shard_map(
        local,
        mesh=mesh,
        in_specs=placed,
        out_specs=(P(("row", "col"), None), P(), P(None, ("row", "col"), None)),
        check_vma=False,
    )
```

profile of v0, /device:TPU:0, one launch (start us, length us, event | category | flops | bytes accessed | tf_op | source)
XLA Modules:
  0.0 753.6 jit_solution(5552647281780713797)
XLA Ops:
  9.3 8.2 %all-to-all-start = ((s32[16,1,2]{2,1,0:T(1,128)}), s32[16,1,2]{2,1,0:T(1,128)}, u32[]{:S(2)}, u32[]{:S(2)}) async-start(s32[16,1,2]{2,1,0:T(1,128)} %copy.29), calls=%async_computation | async-start | bytes 16384 | tf_op jit(solution)/shard_map/all_to_all | solution.py:39
  20.5 22.3 %copy.23 = bf16[1,1,512,128,128]{3,4,2,1,0:T(8,128)(2,1)} copy(bf16[1,1,512,128,128]{4,3,2,1,0:T(8,128)(2,1)} %param.11) | data formatting | bytes 33554432 | tf_op args[1]
  42.9 51.4 %all-gather.2.cloned.1.call-done = bf16[2,16384,256]{2,1,0:T(8,128)(2,1)} async-done(((bf16[2,128,256]{2,1,0:T(8,128)(2,1)}), bf16[2,16384,256]{2,1,0:T(8,128)(2,1)}) %all-gather.2.cloned.1.call-update) | async-done | bytes 16777232 | tf_op jit(solution)/shard_map/all_gather | solution.py:40
  94.3 25.6 %reshape.103 = bf16[256,32768]{1,0:T(8,128)(2,1)} reshape(bf16[2,16384,256]{2,1,0:T(8,128)(2,1)} %all-gather.2.cloned.1.call-done) | data formatting | bytes 33554432 | tf_op jit(solution)/shard_map/reshape | solution.py:42
  119.9 10.1 %convolution_convert_fusion.2 = bf16[32,32768]{1,0:T(8,128)(2,1)} fusion(bf16[256,32768]{1,0:T(8,128)(2,1)} %reshape.103, s32[32]{0:T(128)S(1)} %fusion.31), kind=kOutput, calls=%fused_computation.28 | convolution fusion | flops 537927680 | bytes 18874496 | tf_op jit(solution)/shard_map/dot_general | solution.py:11
  130.0 162.1 %while.22 = (s32[]{:T(128)}, f32[16,32768]{1,0:T(8,128)S(1)}, s32[8,64]{1,0:T(8,128)S(1)}, bf16[8,64,128,128]{3,2,1,0:T(8,128)(2,1)}, s32[8,64]{1,0:T(8,128)S(1)...) while((s32[]{:T(128)}, f32[16,32768]{1,0:T(8,128)S(1)}, s32[8,64]{1,0:T(8,128)S(1)}, ...), condition=%wide.region_1.2_spmd.clone, body=%wide.region_0.1_spmd.clone.sunk | while | flops 1076890624 | bytes 58722400 | solution.py:75
  130.0 2.9 convolution_convert_fusion.6
  134.0 2.9 fusion.65
  136.8 8.0 %copy.42 = f32[8,8,128,256]{3,1,2,0:T(8,128)} copy(f32[8,8,128,256]{3,2,1,0:T(8,128)S(1)} %bitcast.92) | data formatting | bytes 16777216 | tf_op jit(solution)/shard_map/while
  144.8 5.4 convolution_add_fusion.4
  150.2 2.9 convolution_convert_fusion.6
  154.2 2.9 fusion.65
  157.1 8.0 %copy.42 = f32[8,8,128,256]{3,1,2,0:T(8,128)} copy(f32[8,8,128,256]{3,2,1,0:T(8,128)S(1)} %bitcast.92) | data formatting | bytes 16777216 | tf_op jit(solution)/shard_map/while
  165.0 5.4 convolution_add_fusion.4
  170.5 2.9 convolution_convert_fusion.6
  174.5 2.9 fusion.65
  177.3 8.0 %copy.42 = f32[8,8,128,256]{3,1,2,0:T(8,128)} copy(f32[8,8,128,256]{3,2,1,0:T(8,128)S(1)} %bitcast.92) | data formatting | bytes 16777216 | tf_op jit(solution)/shard_map/while
  185.3 5.4 convolution_add_fusion.4
  190.8 2.9 convolution_convert_fusion.6
  197.6 8.0 %copy.42 = f32[8,8,128,256]{3,1,2,0:T(8,128)} copy(f32[8,8,128,256]{3,2,1,0:T(8,128)S(1)} %bitcast.92) | data formatting | bytes 16777216 | tf_op jit(solution)/shard_map/while
  205.6 5.4 convolution_add_fusion.4
  211.0 2.9 convolution_convert_fusion.6
  217.9 8.0 %copy.42 = f32[8,8,128,256]{3,1,2,0:T(8,128)} copy(f32[8,8,128,256]{3,2,1,0:T(8,128)S(1)} %bitcast.92) | data formatting | bytes 16777216 | tf_op jit(solution)/shard_map/while
  225.8 5.4 convolution_add_fusion.4
  231.3 2.9 convolution_convert_fusion.6
  238.1 8.0 %copy.42 = f32[8,8,128,256]{3,1,2,0:T(8,128)} copy(f32[8,8,128,256]{3,2,1,0:T(8,128)S(1)} %bitcast.92) | data formatting | bytes 16777216 | tf_op jit(solution)/shard_map/while
  246.1 5.4 convolution_add_fusion.4
  251.5 2.9 convolution_convert_fusion.6
  258.4 8.0 %copy.42 = f32[8,8,128,256]{3,1,2,0:T(8,128)} copy(f32[8,8,128,256]{3,2,1,0:T(8,128)S(1)} %bitcast.92) | data formatting | bytes 16777216 | tf_op jit(solution)/shard_map/while
  266.3 5.4 convolution_add_fusion.4
  271.8 2.9 convolution_convert_fusion.6
  278.6 8.0 %copy.42 = f32[8,8,128,256]{3,1,2,0:T(8,128)} copy(f32[8,8,128,256]{3,2,1,0:T(8,128)S(1)} %bitcast.92) | data formatting | bytes 16777216 | tf_op jit(solution)/shard_map/while
  286.6 5.4 convolution_add_fusion.4
  292.7 4.4 fusion.18
  299.1 184.7 %while.23 = (s32[]{:T(128)}, f32[32,32768]{1,0:T(8,128)}, s32[8,64]{1,0:T(8,128)S(1)}, bf16[8,64,128,128]{2,3,1,0:T(8,128)(2,1)}, s32[8,64]{1,0:T(8,128)S(1)}, /...) while((s32[]{:T(128)}, f32[32,32768]{1,0:T(8,128)}, s32[8,64]{1,0:T(8,128)S(1)}, ...), condition=%wide.region_4.5_spmd.clone, body=%wide.region_3.4_spmd.clone.sunk | while | flops 1413483520 | bytes 61868128 | solution.py:100
  304.6 8.0 %copy.44 = f32[8,8,128,256]{3,1,2,0:T(8,128)} copy(f32[8,8,128,256]{3,2,1,0:T(8,128)S(1)} %bitcast.93) | data formatting | bytes 16777216 | tf_op jit(solution)/shard_map/while
  312.5 8.8 %convolution_add_fusion.5 = f32[32,32768]{1,0:T(8,128)} fusion(f32[64,32768]{1,0:T(8,128)} %bitcast.91, f32[32,32768]{1,0:T(8,128)} %get-tuple-element.280, pred[]{:T(512)S(6)} %compare.20, s32[64]{0:T(128)S(1)} %get-tuple-element.246), kind=kOutput, calls=%fused_computation.15.clone.1 | convolution fusion | flops 807405568 | bytes 16777472 | tf_op jit(solution)/shard_map/while/body/eval_jaxpr/dot_general | solution.py:16
  323.7 2.9 fusion.71
  326.6 8.0 %copy.44 = f32[8,8,128,256]{3,1,2,0:T(8,128)} copy(f32[8,8,128,256]{3,2,1,0:T(8,128)S(1)} %bitcast.93) | data formatting | bytes 16777216 | tf_op jit(solution)/shard_map/while
  334.5 10.0 %convolution_add_fusion.5 = f32[32,32768]{1,0:T(8,128)} fusion(f32[64,32768]{1,0:T(8,128)} %bitcast.91, f32[32,32768]{1,0:T(8,128)} %get-tuple-element.280, pred[]{:T(512)S(6)} %compare.20, s32[64]{0:T(128)S(1)} %get-tuple-element.246), kind=kOutput, calls=%fused_computation.15.clone.1 | convolution fusion | flops 807405568 | bytes 16777472 | tf_op jit(solution)/shard_map/while/body/eval_jaxpr/dot_general | solution.py:16
  346.9 2.9 fusion.71
  349.8 8.0 %copy.44 = f32[8,8,128,256]{3,1,2,0:T(8,128)} copy(f32[8,8,128,256]{3,2,1,0:T(8,128)S(1)} %bitcast.93) | data formatting | bytes 16777216 | tf_op jit(solution)/shard_map/while
  357.7 10.0 %convolution_add_fusion.5 = f32[32,32768]{1,0:T(8,128)} fusion(f32[64,32768]{1,0:T(8,128)} %bitcast.91, f32[32,32768]{1,0:T(8,128)} %get-tuple-element.280, pred[]{:T(512)S(6)} %compare.20, s32[64]{0:T(128)S(1)} %get-tuple-element.246), kind=kOutput, calls=%fused_computation.15.clone.1 | convolution fusion | flops 807405568 | bytes 16777472 | tf_op jit(solution)/shard_map/while/body/eval_jaxpr/dot_general | solution.py:16
  370.1 2.9 fusion.71
  373.0 8.0 %copy.44 = f32[8,8,128,256]{3,1,2,0:T(8,128)} copy(f32[8,8,128,256]{3,2,1,0:T(8,128)S(1)} %bitcast.93) | data formatting | bytes 16777216 | tf_op jit(solution)/shard_map/while
  381.0 10.0 %convolution_add_fusion.5 = f32[32,32768]{1,0:T(8,128)} fusion(f32[64,32768]{1,0:T(8,128)} %bitcast.91, f32[32,32768]{1,0:T(8,128)} %get-tuple-element.280, pred[]{:T(512)S(6)} %compare.20, s32[64]{0:T(128)S(1)} %get-tuple-element.246), kind=kOutput, calls=%fused_computation.15.clone.1 | convolution fusion | flops 807405568 | bytes 16777472 | tf_op jit(solution)/shard_map/while/body/eval_jaxpr/dot_general | solution.py:16
  393.4 2.9 fusion.71
  396.2 8.0 %copy.44 = f32[8,8,128,256]{3,1,2,0:T(8,128)} copy(f32[8,8,128,256]{3,2,1,0:T(8,128)S(1)} %bitcast.93) | data formatting | bytes 16777216 | tf_op jit(solution)/shard_map/while
  404.2 10.0 %convolution_add_fusion.5 = f32[32,32768]{1,0:T(8,128)} fusion(f32[64,32768]{1,0:T(8,128)} %bitcast.91, f32[32,32768]{1,0:T(8,128)} %get-tuple-element.280, pred[]{:T(512)S(6)} %compare.20, s32[64]{0:T(128)S(1)} %get-tuple-element.246), kind=kOutput, calls=%fused_computation.15.clone.1 | convolution fusion | flops 807405568 | bytes 16777472 | tf_op jit(solution)/shard_map/while/body/eval_jaxpr/dot_general | solution.py:16
  416.6 2.9 fusion.71
  419.4 8.0 %copy.44 = f32[8,8,128,256]{3,1,2,0:T(8,128)} copy(f32[8,8,128,256]{3,2,1,0:T(8,128)S(1)} %bitcast.93) | data formatting | bytes 16777216 | tf_op jit(solution)/shard_map/while
  427.4 10.0 %convolution_add_fusion.5 = f32[32,32768]{1,0:T(8,128)} fusion(f32[64,32768]{1,0:T(8,128)} %bitcast.91, f32[32,32768]{1,0:T(8,128)} %get-tuple-element.280, pred[]{:T(512)S(6)} %compare.20, s32[64]{0:T(128)S(1)} %get-tuple-element.246), kind=kOutput, calls=%fused_computation.15.clone.1 | convolution fusion | flops 807405568 | bytes 16777472 | tf_op jit(solution)/shard_map/while/body/eval_jaxpr/dot_general | solution.py:16
  439.8 2.9 fusion.71
  442.6 8.0 %copy.44 = f32[8,8,128,256]{3,1,2,0:T(8,128)} copy(f32[8,8,128,256]{3,2,1,0:T(8,128)S(1)} %bitcast.93) | data formatting | bytes 16777216 | tf_op jit(solution)/shard_map/while
  450.6 10.0 %convolution_add_fusion.5 = f32[32,32768]{1,0:T(8,128)} fusion(f32[64,32768]{1,0:T(8,128)} %bitcast.91, f32[32,32768]{1,0:T(8,128)} %get-tuple-element.280, pred[]{:T(512)S(6)} %compare.20, s32[64]{0:T(128)S(1)} %get-tuple-element.246), kind=kOutput, calls=%fused_computation.15.clone.1 | convolution fusion | flops 807405568 | bytes 16777472 | tf_op jit(solution)/shard_map/while/body/eval_jaxpr/dot_general | solution.py:16
  463.0 2.9 fusion.71
  465.8 8.0 %copy.44 = f32[8,8,128,256]{3,1,2,0:T(8,128)} copy(f32[8,8,128,256]{3,2,1,0:T(8,128)S(1)} %bitcast.93) | data formatting | bytes 16777216 | tf_op jit(solution)/shard_map/while
  473.8 10.0 %convolution_add_fusion.5 = f32[32,32768]{1,0:T(8,128)} fusion(f32[64,32768]{1,0:T(8,128)} %bitcast.91, f32[32,32768]{1,0:T(8,128)} %get-tuple-element.280, pred[]{:T(512)S(6)} %compare.20, s32[64]{0:T(128)S(1)} %get-tuple-element.246), kind=kOutput, calls=%fused_computation.15.clone.1 | convolution fusion | flops 807405568 | bytes 16777472 | tf_op jit(solution)/shard_map/while/body/eval_jaxpr/dot_general | solution.py:16
  483.8 5.4 copy.35
  489.2 5.6 all-to-all-start.1
  496.8 61.6 %all-to-all-done.1 = f32[16,2,128,256]{3,2,1,0:T(8,128)} async-done(((f32[16,2,128,256]{3,2,1,0:T(8,128)}), f32[16,2,128,256]{3,2,1,0:T(8,128)}, u32[]{:S(2)}, u32[]{:S(2)}) %all-to-all-start.1) | async-done | bytes 4194336 | tf_op jit(solution)/shard_map/all_to_all | solution.py:101
  558.4 4.6 copy.36
  568.8 30.4 %reduce-scatter.2.cloned.1.call-done = f32[2,128,256]{2,1,0:T(8,128)} async-done(((f32[2,1024,256]{2,1,0:T(8,128)}), f32[2,128,256]{2,1,0:T(8,128)}) %reduce-scatter.2.cloned.1.call-update) | async-done | bytes 262160 | tf_op jit(solution)/shard_map/reduce_scatter | solution.py:111
  600.8 144.5 %all-reduce.2.cloned.1.call-done = f32[256,256]{1,0:T(8,128)} async-done(((f32[256,256]{1,0:T(8,128)}), f32[256,256]{1,0:T(8,128)}) %all-reduce.2.cloned.1.call-update) | async-done | bytes 262160 | tf_op jit(solution)/shard_map/psum | solution.py:82
  (92 shorter events, 63.8 us)
Async XLA Ops:
  7.2 285.5 %copy-start = (bf16[256,256]{1,0:T(8,128)(2,1)S(1)}, bf16[256,256]{1,0:T(8,128)(2,1)}, u32[]{:S(2)}) copy-start(bf16[256,256]{1,0:T(8,128)(2,1)} %param.14) | copy-start | bytes 393220
  7.2 87.1 %all-gather.2.cloned.1.call-start = ((), (), s32[]{:S(2)}) async-start(), calls=%async_computation.3 | async-start | bytes 16908288 | tf_op jit(solution)/shard_map/all_gather | solution.py:40
  9.3 479.9 %all-to-all-start = ((s32[16,1,2]{2,1,0:T(1,128)}), s32[16,1,2]{2,1,0:T(1,128)}, u32[]{:S(2)}, u32[]{:S(2)}) async-start(s32[16,1,2]{2,1,0:T(1,128)} %copy.29), calls=%async_computation | async-start | bytes 16384 | tf_op jit(solution)/shard_map/all_to_all | solution.py:39
  292.7 4.4 copy-start.2
  297.1 1.0 copy-start.4
  489.2 69.2 %all-to-all-start.1 = ((f32[16,2,128,256]{3,2,1,0:T(8,128)}), f32[16,2,128,256]{3,2,1,0:T(8,128)}, u32[]{:S(2)}, u32[]{:S(2)}) async-start(f32[16,2,128,256]{3,2,1,0:T(8,128)} %bitcast.101), calls=%async_computation.1 | async-start | bytes 8388608 | tf_op jit(solution)/shard_map/all_to_all | solution.py:101
  494.8 104.4 %reduce-scatter.2.cloned.1.call-start = ((), (), s32[]{:S(2)}) async-start(), calls=%async_computation.5 | async-start | bytes 2359296 | tf_op jit(solution)/shard_map/reduce_scatter | solution.py:111
  563.0 184.0 %copy-start.1 = (bf16[256,256]{1,0:T(8,128)(2,1)S(1)}, bf16[256,256]{1,0:T(8,128)(2,1)}, u32[]{:S(2)}) copy-start(bf16[256,256]{1,0:T(8,128)(2,1)} %param.14) | copy-start | bytes 393220
  564.8 1.6 copy-start.3
  566.3 179.1 %all-reduce.2.cloned.1.call-start = ((), (), s32[]{:S(2)}) async-start(), calls=%async_computation.4 | async-start | bytes 524288 | tf_op jit(solution)/shard_map/psum | solution.py:82
Sparse Core Ops, SparseCore 0:
  11.0 83.1 all-gather.1
  566.4 32.7 reduce-scatter.1
  604.5 140.7 all-reduce.1
where the time goes:
time: 757 us; the launch traced here: 754 us
  waiting for transfers between devices  289 us (38%)
  matrix products  220 us (29%)
  local copies, waits for them, and re-layouts  212 us (28%)
  starting transfers between devices  13.9 us (2%)
  between operations  13.9 us (2%)
    while x32, local copies, waits for them, and re-layouts  145 us
    psum x1, waiting for transfers between devices, local(): weight_grad = lax.psum(local_wgrad, ('row', 'col'))  145 us
    dot_general x17, matrix products, add_rows(): jnp.dot(placer.T, values, preferred_element_type=jnp.float32, precision=l...  124 us
    all_to_all x1, waiting for transfers between devices, local(): lax.all_to_all(slot_sums.reshape(grid_cols, per_peer, block_size, width),...  61.6 us
    all_gather x1, waiting for transfers between devices, local(): whole = lax.all_gather(features, ('row', 'col'), axis=1, tiled=True)  51.4 us
    dot_general x17, matrix products, select_rows(): return jnp.dot(picker, table, preferred_element_type=jnp.float32)  43.4 us
    unnamed x14, local copies, waits for them, and re-layouts  35 us
    reduce_scatter x1, waiting for transfers between devices, local(): owned = lax.psum_scatter(group_grad, 'row', scatter_dimension=1, tiled=True)  30.4 us
  transfers between devices with their start and end apart: 5, of which 4 were waited for; matrix products, arithmetic and copies ran while one was open for 57% of the time, Pallas kernels for 0%

commit v1 on v0

v1 whole, which is shorter than its diff:
```python
import functools
import math

import jax
import jax.numpy as jnp
from jax import lax
from jax.experimental import pallas as pl
from jax.experimental.pallas import tpu as pltpu
from jax.sharding import PartitionSpec as P

GELU_SCALE = math.sqrt(2 / math.pi)
GELU_CUBE = 0.044715
SMEM = pl.BlockSpec(memory_space=pltpu.SMEM)
VMEM = pl.BlockSpec(memory_space=pltpu.VMEM)
ANY = pl.BlockSpec(memory_space=pl.ANY)


def block(index, size):
    return pl.ds(pl.multiple_of(index * size, size), size)


def cell_lists(out_block, slot, out_blocks, slots):
    count = out_block.shape[0]
    ids = jnp.arange(count, dtype=jnp.int32)
    cell = out_block * slots + slot
    order = cell * count + ids
    place = jnp.sum((order[None, :] < order[:, None]).astype(jnp.int32), axis=1)
    members = jnp.sum(jnp.where(place[None, :] == ids[:, None], ids[None, :], 0), axis=1)
    edges = jnp.arange(out_blocks * slots + 1, dtype=jnp.int32)
    starts = jnp.sum((cell[None, :] < edges[:, None]).astype(jnp.int32), axis=1)
    return starts, members


def densify_kernel(starts, members, a_hbm, d_hbm, a_buf, d_buf, in_sem, out_sem, *, out_blocks, slots):
    count, size, _ = a_hbm.shape
    chunks = in_sem.shape[0]
    step = count // chunks

    def fetch(i):
        part = pl.ds(i * step, step)
        return pltpu.make_async_copy(a_hbm.at[part], a_buf.at[part], in_sem.at[i])

    def put(o):
        rows = block(o, size)
        return pltpu.make_async_copy(d_buf.at[rows], d_hbm.at[rows], out_sem.at[o])

    for i in range(chunks):
        fetch(i).start()
    for i in range(chunks):
        fetch(i).wait()

    def one_row(o, _):
        def one_cell(t, _):
            at = o * slots + t
            total = lax.fori_loop(
                starts[at],
                starts[at + 1],
                lambda k, s: s + a_buf[members[k]].astype(jnp.float32),
                jnp.zeros((size, size), jnp.float32),
            )
            d_buf[block(o, size), block(t, size)] = total.astype(jnp.bfloat16)
            return 0

        lax.fori_loop(0, slots, one_cell, 0)
        put(o).start()
        return 0

    lax.fori_loop(0, out_blocks, one_row, 0)
    for o in range(out_blocks):
        put(o).wait()


def densify(starts, members, edges, out_blocks, slots):
    count, size, _ = edges.shape
    shape = (out_blocks * size, slots * size)
    return pl.pallas_call(
        functools.partial(densify_kernel, out_blocks=out_blocks, slots=slots),
        out_shape=jax.ShapeDtypeStruct(shape, jnp.bfloat16),
        in_specs=[SMEM, SMEM, ANY],
        out_specs=ANY,
        scratch_shapes=[
            pltpu.VMEM(edges.shape, jnp.bfloat16),
            pltpu.VMEM(shape, jnp.bfloat16),
            pltpu.SemaphoreType.DMA((math.gcd(count, 16),)),
            pltpu.SemaphoreType.DMA((out_blocks,)),
        ],
        compiler_params=pltpu.CompilerParams(vmem_limit_bytes=40 << 20),
        cost_estimate=pl.CostEstimate(flops=0, bytes_accessed=4 * edges.size, transcendentals=0),
        name="densify",
    )(starts, members, edges)


def pick_kernel(chooser, *refs):
    pieces, (out, table, in_sem, out_sem) = refs[:-4], refs[-4:]
    each = pieces[0].shape[0]
    fetches = [
        pltpu.make_async_copy(piece, table.at[pl.ds(i * each, each)], in_sem.at[i])
        for i, piece in enumerate(pieces)
    ]
    for copy in fetches:
        copy.start()
    for copy in fetches:
        copy.wait()
    puts = [
        pltpu.make_async_copy(table.at[chooser[n]], out.at[n], out_sem.at[n])
        for n in range(out.shape[0])
    ]
    for copy in puts:
        copy.start()
    for copy in puts:
        copy.wait()


def pick_blocks(chooser, pieces):
    each, size, width = pieces[0].shape
    picks = chooser.shape[0]
    return pl.pallas_call(
        pick_kernel,
        out_shape=jax.ShapeDtypeStruct((picks, size, width), jnp.bfloat16),
        in_specs=[SMEM] + [ANY] * len(pieces),
        out_specs=ANY,
        scratch_shapes=[
            pltpu.VMEM((len(pieces) * each, size, width), jnp.bfloat16),
            pltpu.SemaphoreType.DMA((len(pieces),)),
            pltpu.SemaphoreType.DMA((picks,)),
        ],
        compiler_params=pltpu.CompilerParams(vmem_limit_bytes=8 << 20),
        cost_estimate=pl.CostEstimate(
            flops=0, bytes_accessed=4 * picks * size * width, transcendentals=0
        ),
        name="pick_blocks",
    )(chooser, *pieces)


def layer_kernel(
    d_hbm, table, weight, cotangent, activ, wgrad, slot_grad, d_buf, row_grad, sem, *, row_step, col_step
):
    rows, cols = d_hbm.shape
    steps = rows // row_step
    size = slot_grad.shape[2]
    per_step = col_step // size

    def fetch(i):
        part = block(i, row_step)
        return pltpu.make_async_copy(d_hbm.at[part], d_buf.at[part], sem.at[i])

    for i in range(steps):
        fetch(i).start()
    wgrad[...] = jnp.zeros_like(wgrad)

    def forward(i, _):
        fetch(i).wait()
        part = block(i, row_step)
        agg = jnp.dot(d_buf[part, :], table[...], preferred_element_type=jnp.float32)
        agg = agg.astype(jnp.bfloat16)
        w = weight[...]
        pre = jnp.dot(agg, w, preferred_element_type=jnp.float32)
        square = pre * pre
        tanh = jnp.tanh(GELU_SCALE * (pre + GELU_CUBE * (square * pre)))
        half = 0.5 * (1.0 + tanh)
        activ[part, :] = (pre * half).astype(jnp.bfloat16)
        slope = half + (0.5 * GELU_SCALE) * pre * (1.0 - tanh * tanh) * (
            1.0 + (3 * GELU_CUBE) * square
        )
        pre_grad = (cotangent[part, :].astype(jnp.float32) * slope).astype(jnp.bfloat16)
        wgrad[...] += lax.dot_general(
            agg, pre_grad, (((0,), (0,)), ((), ())), preferred_element_type=jnp.float32
        )
        row_grad[:, part] = lax.dot_general(
            w, pre_grad, (((1,), (1,)), ((), ())), preferred_element_type=jnp.float32
        ).astype(jnp.bfloat16)
        return 0

    lax.fori_loop(0, steps, forward, 0)

    def backward(j, _):
        grad = jnp.dot(
            row_grad[...], d_buf[:, block(j, col_step)], preferred_element_type=jnp.float32
        ).astype(jnp.bfloat16)
        for q in range(per_step):
            slot_grad[j * per_step + q] = grad[:, q * size : (q + 1) * size]
        return 0

    lax.fori_loop(0, cols // col_step, backward, 0)


def layer(dense, table, weight, cotangent, size):
    rows, cols = dense.shape
    width = weight.shape[0]
    row_step, col_step = 4 * size, 4 * size
    return pl.pallas_call(
        functools.partial(layer_kernel, row_step=row_step, col_step=col_step),
        out_shape=(
            jax.ShapeDtypeStruct(cotangent.shape, jnp.bfloat16),
            jax.ShapeDtypeStruct((width, width), jnp.float32),
            jax.ShapeDtypeStruct((cols // size, width, size), jnp.bfloat16),
        ),
        in_specs=[ANY, VMEM, VMEM, VMEM],
        out_specs=(VMEM, VMEM, VMEM),
        scratch_shapes=[
            pltpu.VMEM(dense.shape, jnp.bfloat16),
            pltpu.VMEM((width, rows), jnp.bfloat16),
            pltpu.SemaphoreType.DMA((rows // row_step,)),
        ],
        compiler_params=pltpu.CompilerParams(vmem_limit_bytes=40 << 20),
        cost_estimate=pl.CostEstimate(
            flops=4 * rows * cols * width, bytes_accessed=2 * dense.size, transcendentals=0
        ),
        name="layer",
    )(dense, table, weight, cotangent)


def group_sums_kernel(place, returned, keep, send, total):
    half = keep.shape[0]
    total[...] = jnp.zeros_like(total)

    def add(n, _):
        @pl.when(place[n] >= 0)
        def _():
            total[place[n]] += returned[n].astype(jnp.float32)

        return 0

    lax.fori_loop(0, returned.shape[0], add, 0)
    keep[...] = total[:half]
    send[...] = total[half:].astype(jnp.bfloat16)


def group_sums(place, returned, groups):
    _, width, size = returned.shape
    half = (groups // 2, width, size)
    return pl.pallas_call(
        group_sums_kernel,
        out_shape=(
            jax.ShapeDtypeStruct(half, jnp.float32),
            jax.ShapeDtypeStruct(half, jnp.bfloat16),
        ),
        in_specs=[SMEM, VMEM],
        out_specs=(VMEM, VMEM),
        scratch_shapes=[pltpu.VMEM((groups, width, size), jnp.float32)],
        compiler_params=pltpu.CompilerParams(vmem_limit_bytes=16 << 20),
        cost_estimate=pl.CostEstimate(
            flops=returned.size, bytes_accessed=4 * returned.size, transcendentals=0
        ),
        name="group_sums",
    )(place, returned)


def local(features, adjacency, requests, block_coords, weight, cotangent):
    panels, span, width = features.shape
    size = adjacency.shape[-1]
    grid_rows = lax.axis_size("row")
    grid_cols = lax.axis_size("col")
    chips = grid_rows // 2
    row = lax.axis_index("row")
    chip, core = row // 2, row % 2
    out_blocks = cotangent.shape[0] // size
    wanted = requests[0, 0]
    per_peer = wanted.shape[1]
    slots = grid_cols * per_peer

    def exchange(values, axis):
        return lax.all_to_all(values, axis, split_axis=0, concat_axis=0, tiled=True)

    def to_other_core(values):
        return lax.ppermute(values, "row", [(r, r ^ 1) for r in range(grid_rows)])

    def to_chip_ahead(values, ahead):
        return lax.ppermute(
            values, "row", [(r, (r + 2 * ahead) % grid_rows) for r in range(grid_rows)]
        )

    incoming = exchange(wanted, "col").reshape(-1)
    from_panel, from_row = incoming // grid_rows, incoming % grid_rows
    other = (from_row % 2 != core).astype(jnp.int32)
    behind = (chip - from_row // 2) % chips
    ahead = (from_row // 2 - chip) % chips
    chooser = (other * chips + behind) * panels + from_panel
    chooser = jnp.where(incoming >= 0, chooser, 0)
    place = (other * chips + ahead) * panels + from_panel
    place = jnp.where(incoming >= 0, place, -1)

    mine = [features] + [to_chip_ahead(features, d) for d in range(1, chips)]
    pieces = mine + [to_other_core(piece) for piece in mine]
    sends = pick_blocks(chooser, pieces)
    table = exchange(sends, "col").reshape(slots * size, width)

    coords = block_coords[0, 0]
    starts, members = cell_lists(coords[:, 0], coords[:, 1], out_blocks, slots)
    dense = densify(starts, members, adjacency[0, 0], out_blocks, slots)

    activations, local_wgrad, slot_grad = layer(dense, table, weight, cotangent, size)

    returned = exchange(slot_grad, "col")
    keep, send = group_sums(place, returned, panels * grid_rows)
    chip_sum = keep + to_other_core(send).astype(jnp.float32)
    chip_sum = chip_sum.reshape(chips, panels, width, size)
    owned = chip_sum[0]
    for d in range(1, chips):
        owned = owned + to_chip_ahead(chip_sum[d].astype(jnp.bfloat16), d).astype(jnp.float32)
    feature_grad = jnp.swapaxes(owned, 1, 2).astype(jnp.bfloat16)

    strip = width // grid_cols
    strips = exchange(local_wgrad, "col").reshape(grid_cols, strip, width).sum(0)
    copies = jnp.broadcast_to(strips[None], (grid_rows, strip, width))
    strips = exchange(copies, "row").sum(0)
    copies = jnp.broadcast_to(strips[None], (grid_cols, strip, width))
    weight_grad = exchange(copies, "col").reshape(width, width)
    return (activations, weight_grad, feature_grad)


def solution(mesh):
    placed = (
        P(None, ("row", "col"), None),
        P("row", "col", None, None, None),
        P("row", "col", None, None),
        P("row", "col", None, None),
        P(),
        P(("row", "col"), None),
    )
    return jax.shard_map(
        local,
        mesh=mesh,
        in_specs=placed,
        out_specs=(P(("row", "col"), None), P(), P(None, ("row", "col"), None)),
        check_vma=False,
    )
```

time: 757 us -> 156 us (0.21)
  waiting for transfers between devices: 289 us -> 26.4 us
  matrix products: 220 us -> 0 us
  local copies, waits for them, and re-layouts: 212 us -> 5.11 us
  blocking collectives: 0 us -> 53.1 us
  Pallas kernels: 0 us -> 43.9 us
  between operations: 13.9 us -> 0.85 us
  starting transfers between devices: 13.9 us -> 24 us
    dot_general x53 -> x0, matrix products: 220 us -> none  [the longest x17 124 us: add_rows(): jnp.dot(placer.T, values, preferred_element_type=jnp.float32, precision=l...]
    while x32 -> x0, local copies, waits for them, and re-layouts: 145 us -> none
    psum x1 -> x0, waiting for transfers between devices: 145 us -> none  [local(): weight_grad = lax.psum(local_wgrad, ('row', 'col'))]
    all_to_all x0 -> x3, blocking collectives: none -> 53.1 us  [exchange(): return lax.all_to_all(values, axis, split_axis=0, concat_axis=0, tiled=True)]
    all_gather x1 -> x0, waiting for transfers between devices: 51.4 us -> none  [local(): whole = lax.all_gather(features, ('row', 'col'), axis=1, tiled=True)]
    pallas_call x0 -> x4, Pallas kernels: none -> 43.9 us  [the longest x1 22.1 us: densify(): pl.pallas_call(functools.partial(densify_kernel, out_blocks=out_blocks, s...]
    all_to_all x2 -> x3, waiting for transfers between devices: 61.6 us -> 23.9 us  [exchange(): return lax.all_to_all(values, axis, split_axis=0, concat_axis=0, tiled=True)]
    unnamed x14 -> x10, local copies, waits for them, and re-layouts: 35 us -> 2.4 us
  transfers between devices with their start and end apart: 5 -> 14, of which waited for: 4 -> 7; matrix products, arithmetic and copies ran while one was open for 57% -> 3% of each run, Pallas kernels for 0% -> 14%
where the time goes in v1:
time: 156 us; the launch traced here: 155 us
  blocking collectives  53.1 us (34%)
  Pallas kernels  43.9 us (28%)
  waiting for transfers between devices  26.4 us (17%)
  starting transfers between devices  24 us (15%)
  local copies, waits for them, and re-layouts  5.11 us (3%)
  other arithmetic  1.63 us (1%)
    all_to_all x3, blocking collectives, exchange(): return lax.all_to_all(values, axis, split_axis=0, concat_axis=0, tiled=True)  53.1 us
    all_to_all x3, waiting for transfers between devices, exchange(): return lax.all_to_all(values, axis, split_axis=0, concat_axis=0, tiled=True)  23.9 us
    pallas_call x1, Pallas kernels, densify(): pl.pallas_call(functools.partial(densify_kernel, out_blocks=out_blocks, s...  22.1 us
    pallas_call x1, Pallas kernels, layer(): pl.pallas_call(functools.partial(layer_kernel, row_step=row_step, col_ste...  16.7 us
    all_to_all x3, starting transfers between devices, exchange(): return lax.all_to_all(values, axis, split_axis=0, concat_axis=0, tiled=True)  15.3 us
    ppermute x6, starting transfers between devices, to_chip_ahead(): lax.ppermute(values, 'row', [(r, (r + 2 * ahead) % grid_rows) for r in ra...  7.9 us
    pallas_call x1, Pallas kernels, pick_blocks(): pl.pallas_call(pick_kernel, out_shape=jax.ShapeDtypeStruct((picks, size,...  3.59 us
  transfers between devices with their start and end apart: 14, of which 7 were waited for; matrix products, arithmetic and copies ran while one was open for 3% of the time, Pallas kernels for 14%

profile of v1, /device:TPU:0, one launch (start us, length us, event | category | flops | bytes accessed | tf_op | source)
XLA Modules:
  0.0 155.0 jit_solution(15523957534013417674)
XLA Ops:
  0.6 2.9 %collective-permute-start.2 = (bf16[2,128,256]{2,1,0:T(8,128)(2,1)}, bf16[2,128,256]{2,1,0:T(8,128)(2,1)S(1)}, u32[]{:S(2)}, u32[]{:S(2)}) collective-permute-start(bf16[2,128,256]{2,1,0:T(8,128)(2,1)} %refs_0_.1), channel_id=1, source_target_pairs={{0,96},{16,112},{32,0},{48,16},{64,32},{80,48},{96,64},{112,80},{1... | collective-permute-start | bytes 393224 | tf_op jit(solution)/shard_map/ppermute | solution.py:269
  3.5 0.8 collective-permute-start.1
  4.3 0.9 collective-permute-start
  5.2 0.0 collective-permute-start.3
  5.2 1.4 copy.15
  6.6 8.0 %all-to-all-start = ((s32[16,1,2]{2,1,0:T(1,128)}), s32[16,1,2]{2,1,0:T(1,128)S(1)}, u32[]{:S(2)}, u32[]{:S(2)}) async-start(s32[16,1,2]{2,1,0:T(1,128)} %copy.15), calls=%async_computation | async-start | bytes 16384 | tf_op jit(solution)/shard_map/all_to_all | solution.py:263
  14.7 7.5 %all-to-all-done = s32[16,1,2]{2,1,0:T(1,128)S(1)} async-done(((s32[16,1,2]{2,1,0:T(1,128)}), s32[16,1,2]{2,1,0:T(1,128)S(1)}, u32[]{:S(2)}, u32[]{:S(2)}) %all-to-all-start) | async-done | bytes 160 | tf_op jit(solution)/shard_map/all_to_all | solution.py:263
  22.1 0.5 broadcast.101
  22.6 0.7 reduce.4
  23.3 0.1 reshape.60
  23.4 0.0 collective-permute-done.2.refs_3_
  23.4 0.1 collective-permute-start.6
  23.5 0.0 collective-permute-done.1.refs_2_
  23.5 0.5 collective-permute-start.5
  24.0 0.0 collective-permute-done.refs_1_
  24.0 0.1 collective-permute-start.4
  24.2 0.0 collective-permute-done.3.refs_4_
  24.2 0.7 collective-permute-done.6.refs_7_
  24.9 0.2 collective-permute-done.5.refs_6_
  25.1 0.3 collective-permute-done.4.refs_5_
  25.4 0.0 copy-start
  25.4 0.9 copy-done
  26.3 3.6 %pick_blocks.1 = bf16[32,128,256]{2,1,0:T(8,128)(2,1)} custom-call(s32[32]{0:T(128)S(1)} %compare_select_fusion.12.chooser, bf16[2,128,256]{2,1,0:T(8,128)(2,1)S(1)} %copy-done, bf16[2,128,256]{2,1,0:T(8,128)(2,1)S(1)} %collective-permute-done.refs_1_, bf16[2,128,256]{2,1,0:T(8,128)(2,1)S(1)} %collective-permute-done.1.refs_2_, ...), custom_call_target="tpu_custom_call" | custom-call | bytes 4194304 | tf_op jit(solution)/shard_map/pick_blocks/pallas_call | solution.py:117
  29.9 0.0 copy-start.3
  29.9 3.7 %all-to-all-start.1 = ((bf16[32,128,256]{2,1,0:T(8,128)(2,1)}), bf16[32,128,256]{2,1,0:T(8,128)(2,1)S(1)}, u32[]{:S(2)}, u32[]{:S(2)}) async-start(bf16[32,128,256]{2,1,0:T(8,128)(2,1)} %pick_blocks.1), calls=%async_computation.1 | async-start | bytes 4194304 | tf_op jit(solution)/shard_map/all_to_all | solution.py:263
  33.6 0.0 copy-done.3
  33.7 0.2 convert_reduce_fusion.starts
  33.9 0.2 convert_reduce_fusion.1
  34.1 0.2 select_reduce_fusion.members
  34.3 0.0 copy-start.1
  34.3 0.0 copy-start.2
  34.3 22.1 %densify.1.d_hbm = bf16[2048,4096]{1,0:T(8,128)(2,1)} custom-call(s32[513]{0:T(1024)S(1)} %convert_reduce_fusion.starts, s32[512]{0:T(512)S(1)} %select_reduce_fusion.members, bf16[512,128,128]{2,1,0:T(8,128)(2,1)} %bitcast.12), custom_call_target="tpu_custom_call" | custom-call | bytes 33554432 | tf_op jit(solution)/shard_map/densify/pallas_call | solution.py:76
  56.5 11.2 %all-to-all-done.1 = bf16[32,128,256]{2,1,0:T(8,128)(2,1)S(1)} async-done(((bf16[32,128,256]{2,1,0:T(8,128)(2,1)}), bf16[32,128,256]{2,1,0:T(8,128)(2,1)S(1)}, u32[]{:S(2)}, u32[]{:S(2)}) %all-to-all-start.1) | async-done | bytes 2097184 | tf_op jit(solution)/shard_map/all_to_all | solution.py:263
  67.7 0.0 copy-done.1
  67.7 0.0 copy-done.2
  67.7 16.7 %layer.1 = (bf16[2048,256]{1,0:T(8,128)(2,1)}, f32[256,256]{1,0:T(8,128)S(1)}, bf16[32,256,128]{2,1,0:T(8,128)(2,1)S(1)}) custom-call(bf16[2048,4096]{1,0:T(8,128)(2,1)} %densify.1.d_hbm, bf16[4096,256]{1,0:T(8,128)(2,1)S(1)} %bitcast.10, bf16[256,256]{1,0:T(8,128)(2,1)S(1)} %copy-done.2, bf16[2048,256]{1,0:T(8,128)(2,1)S(1)} %copy-done.1), custom_call_target="tpu_custom_call" | custom-call | flops 8589934592 | bytes 16777216 | tf_op jit(solution)/shard_map/layer/pallas_call | solution.py:191
  84.4 31.3 %all_to_all.38.returned = bf16[32,256,128]{2,1,0:T(8,128)(2,1)S(1)} all-to-all(bf16[32,256,128]{2,1,0:T(8,128)(2,1)S(1)} %get-tuple-element.10), channel_id=1, replica_groups=mesh['row'=8,'col'=16] {'col'}, dimensions={0} | all-to-all | bytes 4194304 | tf_op jit(solution)/shard_map/all_to_all | solution.py:263
  115.8 1.5 group_sums.1
  117.3 0.1 collective-permute-start.7
  117.4 12.3 %all_to_all.39 = f32[16,16,256]{2,1,0:T(8,128)S(1)} all-to-all(f32[16,16,256]{2,1,0:T(8,128)S(1)} %bitcast.11), channel_id=1, replica_groups=mesh['row'=8,'col'=16] {'col'}, dimensions={0} | all-to-all | bytes 524288 | tf_op jit(solution)/shard_map/all_to_all | solution.py:263
  129.7 9.5 %all_to_all.40 = f32[8,16,256]{2,1,0:T(8,128)S(1)} all-to-all(f32[8,16,256]{2,1,0:T(8,128)S(1)} %broadcast_in_dim.21), channel_id=1, replica_groups=mesh['row'=8,'col'=16] {'row'}, dimensions={0} | all-to-all | bytes 262144 | tf_op jit(solution)/shard_map/all_to_all | solution.py:263
  139.2 0.7 broadcast_in_dim.22
  139.9 3.5 %all-to-all-start.4 = ((f32[16,16,256]{2,1,0:T(8,128)}), f32[16,16,256]{2,1,0:T(8,128)S(1)}, u32[]{:S(2)}, u32[]{:S(2)}) async-start(f32[16,16,256]{2,1,0:T(8,128)} %broadcast_in_dim.22), calls=%async_computation.4 | async-start | bytes 524288 | tf_op jit(solution)/shard_map/all_to_all | solution.py:263
  143.5 0.0 collective-permute-done.7
  143.5 0.2 fusion.8
  143.7 0.6 collective-permute-start.8
  144.3 2.7 %collective-permute-start.10 = (bf16[2,256,128]{2,1,0:T(8,128)(2,1)S(1)}, bf16[2,256,128]{2,1,0:T(8,128)(2,1)S(1)}, u32[]{:S(2)}, u32[]{:S(2)}) collective-permute-start(bf16[2,256,128]{2,1,0:T(8,128)(2,1)S(1)} %get-tuple-element.33), channel_id=1, source_target_pairs={{0,96},{16,112},{32,0},{48,16},{64,32},{80,48},{96,64},{112,80},{1... | collective-permute-start | bytes 393224 | tf_op jit(solution)/shard_map/ppermute | solution.py:269
  147.0 0.0 collective-permute-start.9
  147.0 5.2 %all-to-all-done.4 = f32[16,16,256]{2,1,0:T(8,128)S(1)} async-done(((f32[16,16,256]{2,1,0:T(8,128)}), f32[16,16,256]{2,1,0:T(8,128)S(1)}, u32[]{:S(2)}, u32[]{:S(2)}) %all-to-all-start.4) | async-done | bytes 262176 | tf_op jit(solution)/shard_map/all_to_all | solution.py:263
  152.2 0.0 collective-permute-done.8
  152.2 0.0 collective-permute-done.10
  152.2 1.3 collective-permute-done.9
  153.5 0.1 fusion.3
  153.5 0.8 copy.16
  154.3 0.7 copy.18
  (8 shorter events, 0.1 us)
Async XLA Ops:
  0.6 22.8 %collective-permute-start.2 = (bf16[2,128,256]{2,1,0:T(8,128)(2,1)}, bf16[2,128,256]{2,1,0:T(8,128)(2,1)S(1)}, u32[]{:S(2)}, u32[]{:S(2)}) collective-permute-start(bf16[2,128,256]{2,1,0:T(8,128)(2,1)} %refs_0_.1), channel_id=1, source_target_pairs={{0,96},{16,112},{32,0},{48,16},{64,32},{80,48},{96,64},{112,80},{1... | collective-permute-start | bytes 393224 | tf_op jit(solution)/shard_map/ppermute | solution.py:269
  3.5 20.0 %collective-permute-start.1 = (bf16[2,128,256]{2,1,0:T(8,128)(2,1)}, bf16[2,128,256]{2,1,0:T(8,128)(2,1)S(1)}, u32[]{:S(2)}, u32[]{:S(2)}) collective-permute-start(bf16[2,128,256]{2,1,0:T(8,128)(2,1)} %refs_0_.1), channel_id=1, source_target_pairs={{0,64},{16,80},{32,96},{48,112},{64,0},{80,16},{96,32},{112,48},{1... | collective-permute-start | bytes 393224 | tf_op jit(solution)/shard_map/ppermute | solution.py:269
  4.3 19.7 %collective-permute-start = (bf16[2,128,256]{2,1,0:T(8,128)(2,1)}, bf16[2,128,256]{2,1,0:T(8,128)(2,1)S(1)}, u32[]{:S(2)}, u32[]{:S(2)}) collective-permute-start(bf16[2,128,256]{2,1,0:T(8,128)(2,1)} %refs_0_.1), channel_id=1, source_target_pairs={{0,32},{16,48},{32,64},{48,80},{64,96},{80,112},{96,0},{112,16},{1... | collective-permute-start | bytes 393224 | tf_op jit(solution)/shard_map/ppermute | solution.py:269
  5.2 18.9 %collective-permute-start.3 = (bf16[2,128,256]{2,1,0:T(8,128)(2,1)}, bf16[2,128,256]{2,1,0:T(8,128)(2,1)S(1)}, u32[]{:S(2)}, u32[]{:S(2)}) collective-permute-start(bf16[2,128,256]{2,1,0:T(8,128)(2,1)} %refs_0_.1), channel_id=1, source_target_pairs={{0,16},{16,0},{32,48},{48,32},{64,80},{80,64},{96,112},{112,96},{1... | collective-permute-start | bytes 393224 | tf_op jit(solution)/shard_map/ppermute | solution.py:266
  6.6 15.5 %all-to-all-start = ((s32[16,1,2]{2,1,0:T(1,128)}), s32[16,1,2]{2,1,0:T(1,128)S(1)}, u32[]{:S(2)}, u32[]{:S(2)}) async-start(s32[16,1,2]{2,1,0:T(1,128)} %copy.15), calls=%async_computation | async-start | bytes 16384 | tf_op jit(solution)/shard_map/all_to_all | solution.py:263
  23.4 1.4 collective-permute-start.6
  23.5 1.5 collective-permute-start.5
  24.0 1.3 collective-permute-start.4
  25.4 0.9 copy-start
  29.9 3.8 %copy-start.3 = (s32[1,1,512,2]{2,3,1,0:T(2,128)S(1)}, s32[1,1,512,2]{2,3,1,0:T(2,128)}, u32[]{:S(2)}) copy-start(s32[1,1,512,2]{2,3,1,0:T(2,128)} %param.9) | copy-start | bytes 12292
  29.9 37.8 %all-to-all-start.1 = ((bf16[32,128,256]{2,1,0:T(8,128)(2,1)}), bf16[32,128,256]{2,1,0:T(8,128)(2,1)S(1)}, u32[]{:S(2)}, u32[]{:S(2)}) async-start(bf16[32,128,256]{2,1,0:T(8,128)(2,1)} %pick_blocks.1), calls=%async_computation.1 | async-start | bytes 4194304 | tf_op jit(solution)/shard_map/all_to_all | solution.py:263
  34.3 33.4 %copy-start.1 = (bf16[2048,256]{1,0:T(8,128)(2,1)S(1)}, bf16[2048,256]{1,0:T(8,128)(2,1)}, u32[]{:S(2)}) copy-start(bf16[2048,256]{1,0:T(8,128)(2,1)} %cotangent.1) | copy-start | bytes 3145732
  34.3 33.4 %copy-start.2 = (bf16[256,256]{1,0:T(8,128)(2,1)S(1)}, bf16[256,256]{1,0:T(8,128)(2,1)}, u32[]{:S(2)}) copy-start(bf16[256,256]{1,0:T(8,128)(2,1)} %weight.1) | copy-start | bytes 393220
  117.3 26.2 %collective-permute-start.7 = (bf16[8,256,128]{2,1,0:T(8,128)(2,1)S(1)}, bf16[8,256,128]{2,1,0:T(8,128)(2,1)S(1)}, u32[]{:S(2)}, u32[]{:S(2)}) collective-permute-start(bf16[8,256,128]{2,1,0:T(8,128)(2,1)S(1)} %get-tuple-element.12), channel_id=1, source_target_pairs={{0,16},{16,0},{32,48},{48,32},{64,80},{80,64},{96,112},{112,96},{1... | collective-permute-start | bytes 1572872 | tf_op jit(solution)/shard_map/ppermute | solution.py:266
  139.9 12.3 %all-to-all-start.4 = ((f32[16,16,256]{2,1,0:T(8,128)}), f32[16,16,256]{2,1,0:T(8,128)S(1)}, u32[]{:S(2)}, u32[]{:S(2)}) async-start(f32[16,16,256]{2,1,0:T(8,128)} %broadcast_in_dim.22), calls=%async_computation.4 | async-start | bytes 524288 | tf_op jit(solution)/shard_map/all_to_all | solution.py:263
  143.7 8.5 %collective-permute-start.8 = (bf16[2,256,128]{2,1,0:T(8,128)(2,1)S(1)}, bf16[2,256,128]{2,1,0:T(8,128)(2,1)S(1)}, u32[]{:S(2)}, u32[]{:S(2)}) collective-permute-start(bf16[2,256,128]{2,1,0:T(8,128)(2,1)S(1)} %get-tuple-element.32), channel_id=1, source_target_pairs={{0,32},{16,48},{32,64},{48,80},{64,96},{80,112},{96,0},{112,16},{1... | collective-permute-start | bytes 393224 | tf_op jit(solution)/shard_map/ppermute | solution.py:269
  144.3 7.9 %collective-permute-start.10 = (bf16[2,256,128]{2,1,0:T(8,128)(2,1)S(1)}, bf16[2,256,128]{2,1,0:T(8,128)(2,1)S(1)}, u32[]{:S(2)}, u32[]{:S(2)}) collective-permute-start(bf16[2,256,128]{2,1,0:T(8,128)(2,1)S(1)} %get-tuple-element.33), channel_id=1, source_target_pairs={{0,96},{16,112},{32,0},{48,16},{64,32},{80,48},{96,64},{112,80},{1... | collective-permute-start | bytes 393224 | tf_op jit(solution)/shard_map/ppermute | solution.py:269
  147.0 6.5 %collective-permute-start.9 = (bf16[2,256,128]{2,1,0:T(8,128)(2,1)S(1)}, bf16[2,256,128]{2,1,0:T(8,128)(2,1)S(1)}, u32[]{:S(2)}, u32[]{:S(2)}) collective-permute-start(bf16[2,256,128]{2,1,0:T(8,128)(2,1)S(1)} %get-tuple-element.34), channel_id=1, source_target_pairs={{0,64},{16,80},{32,96},{48,112},{64,0},{80,16},{96,32},{112,48},{1... | collective-permute-start | bytes 393224 | tf_op jit(solution)/shard_map/ppermute | solution.py:269

commit v2 on v1

v2 whole, which is shorter than its diff:
```python
import functools
import math

import jax
import jax.numpy as jnp
from jax import lax
from jax.experimental import pallas as pl
from jax.experimental.pallas import tpu as pltpu
from jax.sharding import PartitionSpec as P

GELU_SCALE = math.sqrt(2 / math.pi)
GELU_CUBE = 0.044715
SMEM = pl.BlockSpec(memory_space=pltpu.SMEM)
VMEM = pl.BlockSpec(memory_space=pltpu.VMEM)
ANY = pl.BlockSpec(memory_space=pl.ANY)


def block(index, size):
    return pl.ds(pl.multiple_of(index * size, size), size)


def cell_lists(out_block, slot, out_blocks, slots):
    count = out_block.shape[0]
    ids = jnp.arange(count, dtype=jnp.int32)
    cell = out_block * slots + slot
    order = cell * count + ids
    place = jnp.sum((order[None, :] < order[:, None]).astype(jnp.int32), axis=1)
    members = jnp.sum(jnp.where(place[None, :] == ids[:, None], ids[None, :], 0), axis=1)
    edges = jnp.arange(out_blocks * slots + 1, dtype=jnp.int32)
    starts = jnp.sum((cell[None, :] < edges[:, None]).astype(jnp.int32), axis=1)
    return starts, members


def densify_kernel(starts, members, a_hbm, *refs, out_blocks, slots, core):
    d_hbm, a_buf, d_buf, in_sem, out_sem = refs[-5:]
    count, size, _ = a_hbm.shape
    chunks = in_sem.shape[0]
    step = count // chunks

    def fetch(i):
        part = pl.ds(i * step, step)
        return pltpu.make_async_copy(a_hbm.at[part], a_buf.at[part], in_sem.at[i])

    def put(o):
        rows = block(o, size)
        return pltpu.make_async_copy(d_buf.at[rows], d_hbm.at[rows], out_sem.at[o])

    @pl.when(lax.axis_index("row") % 2 == core)
    def _():
        for i in range(chunks):
            fetch(i).start()
        for i in range(chunks):
            fetch(i).wait()

        def one_row(o, _):
            def one_cell(t, _):
                at = o * slots + t
                total = lax.fori_loop(
                    starts[at],
                    starts[at + 1],
                    lambda k, s: s + a_buf[members[k]].astype(jnp.float32),
                    jnp.zeros((size, size), jnp.float32),
                )
                d_buf[block(o, size), block(t, size)] = total.astype(jnp.bfloat16)
                return 0

            lax.fori_loop(0, slots, one_cell, 0)
            put(o).start()
            return 0

        lax.fori_loop(0, out_blocks, one_row, 0)
        for o in range(out_blocks):
            put(o).wait()


def densify(starts, members, edges, out_blocks, slots, core, before=()):
    count, size, _ = edges.shape
    shape = (out_blocks * size, slots * size)
    return pl.pallas_call(
        functools.partial(densify_kernel, out_blocks=out_blocks, slots=slots, core=core),
        out_shape=jax.ShapeDtypeStruct(shape, jnp.bfloat16),
        in_specs=[SMEM, SMEM, ANY] + [ANY] * len(before),
        out_specs=ANY,
        input_output_aliases={3 + i: i for i in range(len(before))},
        scratch_shapes=[
            pltpu.VMEM(edges.shape, jnp.bfloat16),
            pltpu.VMEM(shape, jnp.bfloat16),
            pltpu.SemaphoreType.DMA((math.gcd(count, 16),)),
            pltpu.SemaphoreType.DMA((out_blocks,)),
        ],
        compiler_params=pltpu.CompilerParams(vmem_limit_bytes=40 << 20),
        cost_estimate=pl.CostEstimate(flops=0, bytes_accessed=4 * edges.size, transcendentals=0),
        name="densify",
    )(starts, members, edges, *before)


def block_place(wanted, row, chips, panels, ahead):
    panel, owner = wanted // (2 * chips), wanted % (2 * chips)
    way = owner // 2 - row // 2
    distance = (way if ahead else -way) % chips
    return ((owner % 2 != row % 2).astype(jnp.int32) * chips + distance) * panels + panel


def pick_kernel(incoming, *refs):
    pieces, (out, table, in_sem, out_sem) = refs[:-4], refs[-4:]
    each = pieces[0].shape[0]
    peers, per_peer = incoming.shape
    row = lax.axis_index("row")
    fetches = [
        pltpu.make_async_copy(piece, table.at[pl.ds(i * each, each)], in_sem.at[i])
        for i, piece in enumerate(pieces)
    ]
    for copy in fetches:
        copy.start()
    for copy in fetches:
        copy.wait()
    puts = []
    for n in range(out.shape[0]):
        wanted = jnp.maximum(incoming[n // per_peer, n % per_peer], 0)
        at = block_place(wanted, row, len(pieces) // 2, each, False)
        puts.append(pltpu.make_async_copy(table.at[at], out.at[n], out_sem.at[n]))
    for copy in puts:
        copy.start()
    for copy in puts:
        copy.wait()


def pick_blocks(incoming, pieces):
    each, size, width = pieces[0].shape
    picks = incoming.size
    return pl.pallas_call(
        pick_kernel,
        out_shape=jax.ShapeDtypeStruct((picks, size, width), jnp.bfloat16),
        in_specs=[SMEM] + [ANY] * len(pieces),
        out_specs=ANY,
        scratch_shapes=[
            pltpu.VMEM((len(pieces) * each, size, width), jnp.bfloat16),
            pltpu.SemaphoreType.DMA((len(pieces),)),
            pltpu.SemaphoreType.DMA((picks,)),
        ],
        compiler_params=pltpu.CompilerParams(vmem_limit_bytes=8 << 20),
        cost_estimate=pl.CostEstimate(
            flops=0, bytes_accessed=4 * picks * size * width, transcendentals=0
        ),
        name="pick_blocks",
    )(incoming, *pieces)


def layer_kernel(
    dense, table, weight, cotangent, activ, grads,
    d_buf, act_buf, grad_buf, wgrad, row_grad, d_sem, act_sem, grad_sem,
):
    rows, cols = dense.shape
    peers, _, size = grads.shape
    width = weight.shape[0]
    steps = act_sem.shape[0]
    row_step = rows // steps
    col_step = cols // grad_sem.shape[0]
    per_peer = cols // size // peers
    peers_done = col_step // size // per_peer

    def fetch(i):
        part = block(i, row_step)
        return pltpu.make_async_copy(dense.at[part], d_buf.at[part], d_sem.at[i])

    def put_activ(i):
        part = block(i, row_step)
        return pltpu.make_async_copy(act_buf.at[part], activ.at[part], act_sem.at[i])

    def put_grads(j):
        part = pl.ds(j * peers_done, peers_done)
        return pltpu.make_async_copy(grad_buf.at[part], grads.at[part], grad_sem.at[j])

    for i in range(steps):
        fetch(i).start()
    wgrad[...] = jnp.zeros_like(wgrad)

    def forward(i, _):
        fetch(i).wait()
        part = block(i, row_step)
        agg = jnp.dot(d_buf[part, :], table[...], preferred_element_type=jnp.float32)
        agg = agg.astype(jnp.bfloat16)
        w = weight[...]
        pre = jnp.dot(agg, w, preferred_element_type=jnp.float32)
        square = pre * pre
        tanh = jnp.tanh(GELU_SCALE * (pre + GELU_CUBE * (square * pre)))
        half = 0.5 * (1.0 + tanh)
        act_buf[part, :] = (pre * half).astype(jnp.bfloat16)
        slope = half + (0.5 * GELU_SCALE) * pre * (1.0 - tanh * tanh) * (
            1.0 + (3 * GELU_CUBE) * square
        )
        pre_grad = (cotangent[part, :].astype(jnp.float32) * slope).astype(jnp.bfloat16)
        wgrad[...] += lax.dot_general(
            agg, pre_grad, (((0,), (0,)), ((), ())), preferred_element_type=jnp.float32
        )
        row_grad[:, part] = lax.dot_general(
            w, pre_grad, (((1,), (1,)), ((), ())), preferred_element_type=jnp.float32
        ).astype(jnp.bfloat16)
        put_activ(i).start()
        return 0

    lax.fori_loop(0, steps, forward, 0)

    strip = width // peers
    for p in range(peers):
        rows_of_p = wgrad[p * strip : (p + 1) * strip, :].astype(jnp.bfloat16)
        for q in range(width // size):
            at = per_peer * width + q * strip
            grad_buf[p, at : at + strip] = rows_of_p[:, q * size : (q + 1) * size]

    def backward(j, _):
        grad = jnp.dot(
            row_grad[...], d_buf[:, block(j, col_step)], preferred_element_type=jnp.float32
        ).astype(jnp.bfloat16)
        for p in range(peers_done):
            for q in range(per_peer):
                at = (p * per_peer + q) * size
                grad_buf[j * peers_done + p, q * width : (q + 1) * width] = grad[:, at : at + size]
        put_grads(j).start()
        return 0

    lax.fori_loop(0, cols // col_step, backward, 0)
    for i in range(steps):
        put_activ(i).wait()
    for j in range(cols // col_step):
        put_grads(j).wait()


def layer(dense, table, weight, cotangent, size, peers):
    rows, cols = dense.shape
    width = weight.shape[0]
    sent_rows = cols // size // peers * width + width // peers * (width // size)
    row_step, col_step = 4 * size, 4 * size
    grads = jax.ShapeDtypeStruct((peers, sent_rows, size), jnp.bfloat16)
    return pl.pallas_call(
        layer_kernel,
        out_shape=(jax.ShapeDtypeStruct(cotangent.shape, jnp.bfloat16), grads),
        in_specs=[ANY, VMEM, VMEM, VMEM],
        out_specs=(ANY, ANY),
        scratch_shapes=[
            pltpu.VMEM(dense.shape, jnp.bfloat16),
            pltpu.VMEM(cotangent.shape, jnp.bfloat16),
            pltpu.VMEM(grads.shape, jnp.bfloat16),
            pltpu.VMEM((width, width), jnp.float32),
            pltpu.VMEM((width, rows), jnp.bfloat16),
            pltpu.SemaphoreType.DMA((rows // row_step,)),
            pltpu.SemaphoreType.DMA((rows // row_step,)),
            pltpu.SemaphoreType.DMA((cols // col_step,)),
        ],
        compiler_params=pltpu.CompilerParams(vmem_limit_bytes=40 << 20),
        cost_estimate=pl.CostEstimate(
            flops=4 * rows * cols * width, bytes_accessed=2 * dense.size, transcendentals=0
        ),
        name="layer",
    )(dense, table, weight, cotangent)


def group_sums_kernel(incoming, returned, keep, send, total):
    half, width, _ = keep.shape
    peers, per_peer = incoming.shape
    row = lax.axis_index("row")
    chips = lax.axis_size("row") // 2
    total[...] = jnp.zeros_like(total)

    def add(peer, _):
        for j in range(per_peer):
            wanted = incoming[peer, j]

            @pl.when(wanted >= 0)
            def _():
                at = block_place(jnp.maximum(wanted, 0), row, chips, half // chips, True)
                total[at] += returned[peer, j * width : (j + 1) * width].astype(jnp.float32)

        return 0

    lax.fori_loop(0, peers, add, 0)
    keep[...] = total[:half]
    send[...] = total[half:].astype(jnp.bfloat16)


def group_sums(incoming, returned, groups, width):
    size = returned.shape[2]
    half = (groups // 2, width, size)
    return pl.pallas_call(
        group_sums_kernel,
        out_shape=(
            jax.ShapeDtypeStruct(half, jnp.float32),
            jax.ShapeDtypeStruct(half, jnp.bfloat16),
        ),
        in_specs=[SMEM, VMEM],
        out_specs=(VMEM, VMEM),
        scratch_shapes=[pltpu.VMEM((groups, width, size), jnp.float32)],
        compiler_params=pltpu.CompilerParams(vmem_limit_bytes=16 << 20),
        cost_estimate=pl.CostEstimate(
            flops=returned.size, bytes_accessed=4 * returned.size, transcendentals=0
        ),
        name="group_sums",
    )(incoming, returned)


def chip_sums_kernel(keep, arrived, own, *messages):
    panels = own.shape[0]
    for d in range(1 + len(messages)):
        for p in range(panels):
            total = keep[d * panels + p] + arrived[d * panels + p].astype(jnp.float32)
            if d == 0:
                own[p] = total
            else:
                messages[d - 1][p] = total.astype(jnp.bfloat16)


def chip_sums(keep, arrived, chips):
    half, width, size = keep.shape
    each = (half // chips, width, size)
    shapes = [jax.ShapeDtypeStruct(each, jnp.float32)]
    shapes += [jax.ShapeDtypeStruct(each, jnp.bfloat16)] * (chips - 1)
    return pl.pallas_call(
        chip_sums_kernel,
        out_shape=shapes,
        in_specs=[VMEM] * 2,
        out_specs=[VMEM] * chips,
        compiler_params=pltpu.CompilerParams(vmem_limit_bytes=8 << 20),
        cost_estimate=pl.CostEstimate(flops=keep.size, bytes_accessed=8 * keep.size, transcendentals=0),
        name="chip_sums",
    )(keep, arrived)


def owner_sum_kernel(own, *refs):
    parts, out = refs[:-1], refs[-1]
    for p in range(out.shape[0]):
        total = own[p]
        for part in parts:
            total = total + part[p].astype(jnp.float32)
        out[p] = total.T.astype(jnp.bfloat16)


def owner_sum(own, parts):
    panels, width, size = own.shape
    return pl.pallas_call(
        owner_sum_kernel,
        out_shape=jax.ShapeDtypeStruct((panels, size, width), jnp.bfloat16),
        in_specs=[VMEM] * (1 + len(parts)),
        out_specs=VMEM,
        compiler_params=pltpu.CompilerParams(vmem_limit_bytes=8 << 20),
        cost_estimate=pl.CostEstimate(flops=own.size, bytes_accessed=8 * own.size, transcendentals=0),
        name="owner_sum",
    )(own, *parts)


def local(features, adjacency, requests, block_coords, weight, cotangent):
    panels, span, width = features.shape
    size = adjacency.shape[-1]
    grid_rows = lax.axis_size("row")
    grid_cols = lax.axis_size("col")
    chips = grid_rows // 2
    out_blocks = cotangent.shape[0] // size
    wanted = requests[0, 0]
    per_peer = wanted.shape[1]
    slots = grid_cols * per_peer

    def exchange(values, axis):
        return lax.all_to_all(values, axis, split_axis=0, concat_axis=0, tiled=True)

    def to_other_core(values):
        return lax.ppermute(values, "row", [(r, r ^ 1) for r in range(grid_rows)])

    def to_chip_ahead(values, ahead):
        return lax.ppermute(
            values, "row", [(r, (r + 2 * ahead) % grid_rows) for r in range(grid_rows)]
        )

    incoming = exchange(wanted, "col")
    mine = [features] + [to_chip_ahead(features, d) for d in range(1, chips)]
    incoming, *mine = lax.optimization_barrier((incoming, *mine))
    pieces = mine + [to_other_core(piece) for piece in mine]
    sends = pick_blocks(incoming, pieces)

    coords = block_coords[0, 0]
    starts, members = cell_lists(coords[:, 0], coords[:, 1], out_blocks, slots)
    edges = adjacency[0, 0]
    dense = densify(starts, members, edges, out_blocks, slots, 1)
    sends, dense = lax.optimization_barrier((sends, dense))
    table = exchange(sends, "col").reshape(slots * size, width)
    dense = densify(starts, members, edges, out_blocks, slots, 0, (dense,))

    activations, grads = layer(dense, table, weight, cotangent, size, grid_cols)

    returned = exchange(grads, "col")
    strip = jnp.sum(returned[:, per_peer * width :].astype(jnp.float32), axis=0)

    strip = strip + to_other_core(strip)
    near = [strip] + [to_chip_ahead(strip, d) for d in range(1, chips)]
    strip = sum(near[2::2], near[0]) + sum(near[3::2], near[1])

    keep, send = group_sums(incoming, returned, panels * grid_rows, width)
    own, *messages = chip_sums(keep, to_other_core(send), chips)
    strip, *messages = lax.optimization_barrier((strip, *messages))
    parts = [to_chip_ahead(message, d + 1) for d, message in enumerate(messages)]
    feature_grad = owner_sum(own, parts)

    copies = jnp.broadcast_to(strip[None], (grid_cols, *strip.shape))
    strips = exchange(copies, "col").reshape(grid_cols, width // size, width // grid_cols, size)
    weight_grad = jnp.swapaxes(strips, 1, 2).reshape(width, width)
    return (activations, weight_grad, feature_grad)


def solution(mesh):
    placed = (
        P(None, ("row", "col"), None),
        P("row", "col", None, None, None),
        P("row", "col", None, None),
        P("row", "col", None, None),
        P(),
        P(("row", "col"), None),
    )
    return jax.shard_map(
        local,
        mesh=mesh,
        in_specs=placed,
        out_specs=(P(("row", "col"), None), P(), P(None, ("row", "col"), None)),
        check_vma=False,
    )
```

time: 156 us -> 139 us (0.89)
  blocking collectives: 53.1 us -> 26.4 us
  starting transfers between devices: 24 us -> 41.7 us
  waiting for transfers between devices: 26.4 us -> 18.6 us
  Pallas kernels: 43.9 us -> 46.6 us
  local copies, waits for them, and re-layouts: 5.11 us -> 3.12 us
    all_to_all x3 -> x1, blocking collectives: 53.1 us -> 26.4 us  [exchange(): return lax.all_to_all(values, axis, split_axis=0, concat_axis=0, tiled=True)]
    all_to_all x3, waiting for transfers between devices: 23.9 us -> 6.46 us  [exchange(): return lax.all_to_all(values, axis, split_axis=0, concat_axis=0, tiled=True)]
    ppermute x5 -> x6, starting transfers between devices: 0.76 us -> 14.6 us  [to_other_core(): return lax.ppermute(values, 'row', [(r, r ^ 1) for r in range(grid_rows)])]
    ppermute x6 -> x9, waiting for transfers between devices: 1.27 us -> 10.7 us  [to_chip_ahead(): lax.ppermute(values, 'row', [(r, (r + 2 * ahead) % grid_rows) for r in ra...]
    ppermute x6 -> x9, starting transfers between devices: 7.9 us -> 11.8 us  [to_chip_ahead(): lax.ppermute(values, 'row', [(r, (r + 2 * ahead) % grid_rows) for r in ra...]
    unnamed x10 -> x7, local copies, waits for them, and re-layouts: 2.4 us -> 0.74 us
    pallas_call x1 -> x3, Pallas kernels: 16.7 us -> 17.8 us  [the longest x1 16.9 us: layer(): pl.pallas_call(layer_kernel, out_shape=(jax.ShapeDtypeStruct(cotangent.sh...]
    pallas_call x1 -> x2, Pallas kernels: 22.1 us -> 23.1 us  [densify(): pl.pallas_call(functools.partial(densify_kernel, out_blocks=out_blocks, s...]
  transfers between devices with their start and end apart: 14 -> 18, of which waited for: 7 -> 7; matrix products, arithmetic and copies ran while one was open for 3% -> 2% of each run, Pallas kernels for 14% -> 17%
where the time goes in v2:
time: 139 us
  Pallas kernels  46.6 us (34%)
  starting transfers between devices  41.7 us (30%)
  blocking collectives  26.4 us (19%)
  waiting for transfers between devices  18.6 us (13%)
  local copies, waits for them, and re-layouts  3.12 us (2%)
  other arithmetic  1.45 us (1%)
    all_to_all x1, blocking collectives, exchange(): return lax.all_to_all(values, axis, split_axis=0, concat_axis=0, tiled=True)  26.4 us
    pallas_call x2, Pallas kernels, densify(): pl.pallas_call(functools.partial(densify_kernel, out_blocks=out_blocks, s...  23.1 us
    pallas_call x1, Pallas kernels, layer(): pl.pallas_call(layer_kernel, out_shape=(jax.ShapeDtypeStruct(cotangent.sh...  16.9 us
    all_to_all x3, starting transfers between devices, exchange(): return lax.all_to_all(values, axis, split_axis=0, concat_axis=0, tiled=True)  15.3 us
    ppermute x6, starting transfers between devices, to_other_core(): return lax.ppermute(values, 'row', [(r, r ^ 1) for r in range(grid_rows)])  14.6 us
    ppermute x9, starting transfers between devices, to_chip_ahead(): lax.ppermute(values, 'row', [(r, (r + 2 * ahead) % grid_rows) for r in ra...  11.8 us
    ppermute x9, waiting for transfers between devices, to_chip_ahead(): lax.ppermute(values, 'row', [(r, (r + 2 * ahead) % grid_rows) for r in ra...  10.7 us
    all_to_all x3, waiting for transfers between devices, exchange(): return lax.all_to_all(values, axis, split_axis=0, concat_axis=0, tiled=True)  6.46 us
  transfers between devices with their start and end apart: 18, of which 7 were waited for; matrix products, arithmetic and copies ran while one was open for 2% of the time, Pallas kernels for 17%

profile of v2, /device:TPU:0, one launch (start us, length us, event | category | flops | bytes accessed | tf_op | source)
XLA Modules:
  0.0 138.7 jit_solution(16034389611574504609)
XLA Ops:
  0.6 3.2 %collective-permute-start.1 = (bf16[2,128,256]{2,1,0:T(8,128)(2,1)}, bf16[2,128,256]{2,1,0:T(8,128)(2,1)S(1)}, u32[]{:S(2)}, u32[]{:S(2)}) collective-permute-start(bf16[2,128,256]{2,1,0:T(8,128)(2,1)} %refs_0_), channel_id=1, source_target_pairs={{0,64},{16,80},{32,96},{48,112},{64,0},{80,16},{96,32},{112,48},{1... | collective-permute-start | bytes 393224 | tf_op jit(solution)/shard_map/ppermute | solution.py:368
  3.8 0.6 collective-permute-start
  4.4 2.6 %collective-permute-start.2 = (bf16[2,128,256]{2,1,0:T(8,128)(2,1)}, bf16[2,128,256]{2,1,0:T(8,128)(2,1)S(1)}, u32[]{:S(2)}, u32[]{:S(2)}) collective-permute-start(bf16[2,128,256]{2,1,0:T(8,128)(2,1)} %refs_0_), channel_id=1, source_target_pairs={{0,96},{16,112},{32,0},{48,16},{64,32},{80,48},{96,64},{112,80},{1... | collective-permute-start | bytes 393224 | tf_op jit(solution)/shard_map/ppermute | solution.py:368
  7.1 1.4 copy.22
  8.4 8.0 %all-to-all-start = ((s32[16,1,2]{2,1,0:T(1,128)}), s32[16,1,2]{2,1,0:T(1,128)S(1)}, u32[]{:S(2)}, u32[]{:S(2)}) async-start(s32[16,1,2]{2,1,0:T(1,128)} %copy.22), calls=%async_computation | async-start | bytes 16384 | tf_op jit(solution)/shard_map/all_to_all | solution.py:362
  16.5 0.8 iota_add_fusion
  17.2 0.2 convert_reduce_fusion.1
  17.5 6.5 %all-to-all-done = s32[16,1,2]{2,1,0:T(1,128)S(1)} async-done(((s32[16,1,2]{2,1,0:T(1,128)}), s32[16,1,2]{2,1,0:T(1,128)S(1)}, u32[]{:S(2)}, u32[]{:S(2)}) %all-to-all-start) | async-done | bytes 160 | tf_op jit(solution)/shard_map/all_to_all | solution.py:362
  23.9 0.1 copy.23
  24.0 0.0 collective-permute-done.1.refs_2_
  24.0 0.0 collective-permute-done.refs_1_
  24.0 0.0 collective-permute-done.2.refs_3_
  24.0 0.1 collective-permute-start.3
  24.1 0.5 collective-permute-start.4
  24.6 0.1 collective-permute-start.5
  24.7 0.4 collective-permute-start.6
  25.1 0.2 select_reduce_fusion.members
  25.3 0.2 convert_reduce_fusion.starts
  25.5 0.0 copy-start
  25.5 0.9 densify.2.refs_0_
  26.5 0.1 copy.24.incoming
  26.5 0.0 collective-permute-done.3.refs_4_
  26.5 0.0 collective-permute-done.4.refs_5_
  26.5 0.0 collective-permute-done.5.refs_6_
  26.6 0.0 collective-permute-done.6.refs_7_
  26.6 0.0 copy-done
  26.6 3.7 %pick_blocks.1 = bf16[32,128,256]{2,1,0:T(8,128)(2,1)} custom-call(s32[16,2]{1,0:T(8,128)S(1)} %copy.24.incoming, bf16[2,128,256]{2,1,0:T(8,128)(2,1)S(1)} %copy-done, bf16[2,128,256]{2,1,0:T(8,128)(2,1)S(1)} %collective-permute-done.refs_1_, bf16[2,128,256]{2,1,0:T(8,128)(2,1)S(1)} %collective-permute-done.1.refs_2_, ...), custom_call_target="tpu_custom_call" | custom-call | bytes 4194304 | tf_op jit(solution)/shard_map/pick_blocks/pallas_call | solution.py:131
  30.3 3.7 %all-to-all-start.1 = ((bf16[32,128,256]{2,1,0:T(8,128)(2,1)}), bf16[32,128,256]{2,1,0:T(8,128)(2,1)S(1)}, u32[]{:S(2)}, u32[]{:S(2)}) async-start(bf16[32,128,256]{2,1,0:T(8,128)(2,1)} %pick_blocks.1), calls=%async_computation.1 | async-start | bytes 4194304 | tf_op jit(solution)/shard_map/all_to_all | solution.py:362
  34.1 0.0 copy-start.1
  34.1 0.0 copy-start.2
  34.1 22.2 %densify.3.dense = bf16[2048,4096]{1,0:T(8,128)(2,1)} custom-call(s32[513]{0:T(1024)S(1)} %convert_reduce_fusion.starts, s32[512]{0:T(512)S(1)} %select_reduce_fusion.members, bf16[512,128,128]{2,1,0:T(8,128)(2,1)} %bitcast.17, bf16[2048,4096]{1,0:T(8,128)(2,1)} %densify.2.refs_0_), custom_call_target="tpu_custom_call", output_to_operand_aliasing={{}: (3, {})} | custom-call | bytes 33554432 | tf_op jit(solution)/shard_map/densify/pallas_call | solution.py:79
  56.2 0.0 all-to-all-done.1
  56.2 0.0 copy-done.1
  56.3 0.0 copy-done.2
  56.3 16.9 %layer.1 = (bf16[2048,256]{1,0:T(8,128)(2,1)}, bf16[16,544,128]{2,1,0:T(8,128)(2,1)S(1)}) custom-call(bf16[2048,4096]{1,0:T(8,128)(2,1)} %densify.3.dense, bf16[4096,256]{1,0:T(8,128)(2,1)S(1)} %bitcast.15, bf16[256,256]{1,0:T(8,128)(2,1)S(1)} %copy-done.2, bf16[2048,256]{1,0:T(8,128)(2,1)S(1)} %copy-done.1), custom_call_target="tpu_custom_call" | custom-call | flops 8589934592 | bytes 16777216 | tf_op jit(solution)/shard_map/layer/pallas_call | solution.py:235
  73.2 26.4 %all_to_all.27.returned = bf16[16,544,128]{2,1,0:T(8,128)(2,1)S(1)} all-to-all(bf16[16,544,128]{2,1,0:T(8,128)(2,1)S(1)} %get-tuple-element.30), channel_id=1, replica_groups=mesh['row'=8,'col'=16] {'col'}, dimensions={0} | all-to-all | bytes 4456448 | tf_op jit(solution)/shard_map/all_to_all | solution.py:362
  99.6 1.9 %group_sums.1 = (f32[8,256,128]{2,1,0:T(8,128)S(1)}, bf16[8,256,128]{2,1,0:T(8,128)(2,1)S(1)}) custom-call(s32[16,2]{1,0:T(8,128)S(1)} %copy.24.incoming, bf16[16,544,128]{2,1,0:T(8,128)(2,1)S(1)} %all_to_all.27.returned), custom_call_target="tpu_custom_call" | custom-call | flops 1114112 | bytes 4456448 | tf_op jit(solution)/shard_map/group_sums/pallas_call | solution.py:284
  101.5 13.4 %collective-permute-start.11 = (bf16[8,256,128]{2,1,0:T(8,128)(2,1)S(1)}, bf16[8,256,128]{2,1,0:T(8,128)(2,1)S(1)}, u32[]{:S(2)}, u32[]{:S(2)}) collective-permute-start(bf16[8,256,128]{2,1,0:T(8,128)(2,1)S(1)} %get-tuple-element.32), channel_id=1, source_target_pairs={{0,16},{16,0},{32,48},{48,32},{64,80},{80,64},{96,112},{112,96},{1... | collective-permute-start | bytes 1572872 | tf_op jit(solution)/shard_map/ppermute | solution.py:365
  115.0 0.1 collective-permute-start.7
  115.1 1.4 %collective-permute-done.7 = f32[32,128]{1,0:T(8,128)S(1)} collective-permute-done((f32[32,128]{1,0:T(8,128)S(1)}, f32[32,128]{1,0:T(8,128)S(1)}, u32[]{:S(2)}, u32[]{:S(2)}) %collective-permute-start.7) | collective-permute-done | bytes 16416 | tf_op jit(solution)/shard_map/ppermute | solution.py:365
  116.5 0.1 collective-permute-start.10
  116.7 1.9 %collective-permute-start.9 = (f32[32,128]{1,0:T(8,128)S(1)}, f32[32,128]{1,0:T(8,128)S(1)}, u32[]{:S(2)}, u32[]{:S(2)}) collective-permute-start(f32[32,128]{1,0:T(8,128)S(1)} %add.40), channel_id=1, source_target_pairs={{0,32},{16,48},{32,64},{48,80},{64,96},{80,112},{96,0},{112,16},{1... | collective-permute-start | bytes 49160 | tf_op jit(solution)/shard_map/ppermute | solution.py:368
  118.6 0.0 collective-permute-start.8
  118.6 1.7 %collective-permute-done.10 = f32[32,128]{1,0:T(8,128)S(1)} collective-permute-done((f32[32,128]{1,0:T(8,128)S(1)}, f32[32,128]{1,0:T(8,128)S(1)}, u32[]{:S(2)}, u32[]{:S(2)}) %collective-permute-start.10) | collective-permute-done | bytes 16416 | tf_op jit(solution)/shard_map/ppermute | solution.py:368
  120.3 1.3 collective-permute-done.9
  121.6 2.2 %collective-permute-done.8 = f32[32,128]{1,0:T(8,128)S(1)} collective-permute-done((f32[32,128]{1,0:T(8,128)S(1)}, f32[32,128]{1,0:T(8,128)S(1)}, u32[]{:S(2)}, u32[]{:S(2)}) %collective-permute-start.8) | collective-permute-done | bytes 16416 | tf_op jit(solution)/shard_map/ppermute | solution.py:368
  123.8 0.0 collective-permute-done.11.arrived
  123.8 0.1 chip_sums.1
  123.9 0.7 broadcast_in_dim.16
  124.7 3.5 %all-to-all-start.3 = ((f32[16,32,128]{2,1,0:T(8,128)}), f32[16,32,128]{2,1,0:T(8,128)S(1)}, u32[]{:S(2)}, u32[]{:S(2)}) async-start(f32[16,32,128]{2,1,0:T(8,128)} %broadcast_in_dim.16), calls=%async_computation.3 | async-start | bytes 524288 | tf_op jit(solution)/shard_map/all_to_all | solution.py:362
  128.2 0.1 collective-permute-start.12
  128.3 2.8 %collective-permute-start.13 = (bf16[2,256,128]{2,1,0:T(8,128)(2,1)S(1)}, bf16[2,256,128]{2,1,0:T(8,128)(2,1)S(1)}, u32[]{:S(2)}, u32[]{:S(2)}) collective-permute-start(bf16[2,256,128]{2,1,0:T(8,128)(2,1)S(1)} %get-tuple-element.39), channel_id=1, source_target_pairs={{0,64},{16,80},{32,96},{48,112},{64,0},{80,16},{96,32},{112,48},{1... | collective-permute-start | bytes 393224 | tf_op jit(solution)/shard_map/ppermute | solution.py:368
  131.1 0.4 collective-permute-start.14
  131.5 4.8 %collective-permute-done.12.refs_0_ = bf16[2,256,128]{2,1,0:T(8,128)(2,1)S(1)} collective-permute-done((bf16[2,256,128]{2,1,0:T(8,128)(2,1)S(1)}, bf16[2,256,128]{2,1,0:T(8,128)(2,1)S(1)}, u32[]{:S(2)}, u32[]{:S(2)}) %collective-permute-start.12) | collective-permute-done | bytes 131104 | tf_op jit(solution)/shard_map/ppermute | solution.py:368
  136.4 0.0 collective-permute-done.13.refs_1_
  136.4 0.7 collective-permute-done.14.refs_2_
  137.0 0.8 owner_sum.1
  137.8 0.0 all-to-all-done.3
  137.8 0.1 copy.26
  137.9 0.7 copy.29
  (4 shorter events, 0.0 us)
Async XLA Ops:
  0.6 23.4 %collective-permute-start.1 = (bf16[2,128,256]{2,1,0:T(8,128)(2,1)}, bf16[2,128,256]{2,1,0:T(8,128)(2,1)S(1)}, u32[]{:S(2)}, u32[]{:S(2)}) collective-permute-start(bf16[2,128,256]{2,1,0:T(8,128)(2,1)} %refs_0_), channel_id=1, source_target_pairs={{0,64},{16,80},{32,96},{48,112},{64,0},{80,16},{96,32},{112,48},{1... | collective-permute-start | bytes 393224 | tf_op jit(solution)/shard_map/ppermute | solution.py:368
  3.8 20.2 %collective-permute-start = (bf16[2,128,256]{2,1,0:T(8,128)(2,1)}, bf16[2,128,256]{2,1,0:T(8,128)(2,1)S(1)}, u32[]{:S(2)}, u32[]{:S(2)}) collective-permute-start(bf16[2,128,256]{2,1,0:T(8,128)(2,1)} %refs_0_), channel_id=1, source_target_pairs={{0,32},{16,48},{32,64},{48,80},{64,96},{80,112},{96,0},{112,16},{1... | collective-permute-start | bytes 393224 | tf_op jit(solution)/shard_map/ppermute | solution.py:368
  4.4 19.6 %collective-permute-start.2 = (bf16[2,128,256]{2,1,0:T(8,128)(2,1)}, bf16[2,128,256]{2,1,0:T(8,128)(2,1)S(1)}, u32[]{:S(2)}, u32[]{:S(2)}) collective-permute-start(bf16[2,128,256]{2,1,0:T(8,128)(2,1)} %refs_0_), channel_id=1, source_target_pairs={{0,96},{16,112},{32,0},{48,16},{64,32},{80,48},{96,64},{112,80},{1... | collective-permute-start | bytes 393224 | tf_op jit(solution)/shard_map/ppermute | solution.py:368
  8.4 15.5 %all-to-all-start = ((s32[16,1,2]{2,1,0:T(1,128)}), s32[16,1,2]{2,1,0:T(1,128)S(1)}, u32[]{:S(2)}, u32[]{:S(2)}) async-start(s32[16,1,2]{2,1,0:T(1,128)} %copy.22), calls=%async_computation | async-start | bytes 16384 | tf_op jit(solution)/shard_map/all_to_all | solution.py:362
  24.0 2.5 %collective-permute-start.3 = (bf16[2,128,256]{2,1,0:T(8,128)(2,1)}, bf16[2,128,256]{2,1,0:T(8,128)(2,1)S(1)}, u32[]{:S(2)}, u32[]{:S(2)}) collective-permute-start(bf16[2,128,256]{2,1,0:T(8,128)(2,1)} %refs_0_), channel_id=1, source_target_pairs={{0,16},{16,0},{32,48},{48,32},{64,80},{80,64},{96,112},{112,96},{1... | collective-permute-start | bytes 393224 | tf_op jit(solution)/shard_map/ppermute | solution.py:365
  24.1 2.4 %collective-permute-start.4 = (bf16[2,128,256]{2,1,0:T(8,128)(2,1)S(1)}, bf16[2,128,256]{2,1,0:T(8,128)(2,1)S(1)}, u32[]{:S(2)}, u32[]{:S(2)}) collective-permute-start(bf16[2,128,256]{2,1,0:T(8,128)(2,1)S(1)} %collective-permute-done.refs_1_), channel_id=1, source_target_pairs={{0,16},{16,0},{32,48},{48,32},{64,80},{80,64},{96,112},{112,96},{1... | collective-permute-start | bytes 393224 | tf_op jit(solution)/shard_map/ppermute | solution.py:365
  24.6 1.9 %collective-permute-start.5 = (bf16[2,128,256]{2,1,0:T(8,128)(2,1)S(1)}, bf16[2,128,256]{2,1,0:T(8,128)(2,1)S(1)}, u32[]{:S(2)}, u32[]{:S(2)}) collective-permute-start(bf16[2,128,256]{2,1,0:T(8,128)(2,1)S(1)} %collective-permute-done.1.refs_2_), channel_id=1, source_target_pairs={{0,16},{16,0},{32,48},{48,32},{64,80},{80,64},{96,112},{112,96},{1... | collective-permute-start | bytes 393224 | tf_op jit(solution)/shard_map/ppermute | solution.py:365
  24.7 1.8 %collective-permute-start.6 = (bf16[2,128,256]{2,1,0:T(8,128)(2,1)S(1)}, bf16[2,128,256]{2,1,0:T(8,128)(2,1)S(1)}, u32[]{:S(2)}, u32[]{:S(2)}) collective-permute-start(bf16[2,128,256]{2,1,0:T(8,128)(2,1)S(1)} %collective-permute-done.2.refs_3_), channel_id=1, source_target_pairs={{0,16},{16,0},{32,48},{48,32},{64,80},{80,64},{96,112},{112,96},{1... | collective-permute-start | bytes 393224 | tf_op jit(solution)/shard_map/ppermute | solution.py:365
  25.5 1.0 copy-start
  30.3 25.9 %all-to-all-start.1 = ((bf16[32,128,256]{2,1,0:T(8,128)(2,1)}), bf16[32,128,256]{2,1,0:T(8,128)(2,1)S(1)}, u32[]{:S(2)}, u32[]{:S(2)}) async-start(bf16[32,128,256]{2,1,0:T(8,128)(2,1)} %pick_blocks.1), calls=%async_computation.1 | async-start | bytes 4194304 | tf_op jit(solution)/shard_map/all_to_all | solution.py:362
  34.1 22.2 %copy-start.1 = (bf16[2048,256]{1,0:T(8,128)(2,1)S(1)}, bf16[2048,256]{1,0:T(8,128)(2,1)}, u32[]{:S(2)}) copy-start(bf16[2048,256]{1,0:T(8,128)(2,1)} %cotangent.1) | copy-start | bytes 3145732
  34.1 22.2 %copy-start.2 = (bf16[256,256]{1,0:T(8,128)(2,1)S(1)}, bf16[256,256]{1,0:T(8,128)(2,1)}, u32[]{:S(2)}) copy-start(bf16[256,256]{1,0:T(8,128)(2,1)} %weight.1) | copy-start | bytes 393220
  101.5 22.3 %collective-permute-start.11 = (bf16[8,256,128]{2,1,0:T(8,128)(2,1)S(1)}, bf16[8,256,128]{2,1,0:T(8,128)(2,1)S(1)}, u32[]{:S(2)}, u32[]{:S(2)}) collective-permute-start(bf16[8,256,128]{2,1,0:T(8,128)(2,1)S(1)} %get-tuple-element.32), channel_id=1, source_target_pairs={{0,16},{16,0},{32,48},{48,32},{64,80},{80,64},{96,112},{112,96},{1... | collective-permute-start | bytes 1572872 | tf_op jit(solution)/shard_map/ppermute | solution.py:365
  115.0 1.5 %collective-permute-start.7 = (f32[32,128]{1,0:T(8,128)S(1)}, f32[32,128]{1,0:T(8,128)S(1)}, u32[]{:S(2)}, u32[]{:S(2)}) collective-permute-start(f32[32,128]{1,0:T(8,128)S(1)} %convert_reduce_fusion.2), channel_id=1, source_target_pairs={{0,16},{16,0},{32,48},{48,32},{64,80},{80,64},{96,112},{112,96},{1... | collective-permute-start | bytes 49160 | tf_op jit(solution)/shard_map/ppermute | solution.py:365
  116.5 3.8 %collective-permute-start.10 = (f32[32,128]{1,0:T(8,128)S(1)}, f32[32,128]{1,0:T(8,128)S(1)}, u32[]{:S(2)}, u32[]{:S(2)}) collective-permute-start(f32[32,128]{1,0:T(8,128)S(1)} %add.40), channel_id=1, source_target_pairs={{0,96},{16,112},{32,0},{48,16},{64,32},{80,48},{96,64},{112,80},{1... | collective-permute-start | bytes 49160 | tf_op jit(solution)/shard_map/ppermute | solution.py:368
  116.7 4.9 %collective-permute-start.9 = (f32[32,128]{1,0:T(8,128)S(1)}, f32[32,128]{1,0:T(8,128)S(1)}, u32[]{:S(2)}, u32[]{:S(2)}) collective-permute-start(f32[32,128]{1,0:T(8,128)S(1)} %add.40), channel_id=1, source_target_pairs={{0,32},{16,48},{32,64},{48,80},{64,96},{80,112},{96,0},{112,16},{1... | collective-permute-start | bytes 49160 | tf_op jit(solution)/shard_map/ppermute | solution.py:368
  118.6 5.2 %collective-permute-start.8 = (f32[32,128]{1,0:T(8,128)S(1)}, f32[32,128]{1,0:T(8,128)S(1)}, u32[]{:S(2)}, u32[]{:S(2)}) collective-permute-start(f32[32,128]{1,0:T(8,128)S(1)} %add.40), channel_id=1, source_target_pairs={{0,64},{16,80},{32,96},{48,112},{64,0},{80,16},{96,32},{112,48},{1... | collective-permute-start | bytes 49160 | tf_op jit(solution)/shard_map/ppermute | solution.py:368
  124.7 13.1 %all-to-all-start.3 = ((f32[16,32,128]{2,1,0:T(8,128)}), f32[16,32,128]{2,1,0:T(8,128)S(1)}, u32[]{:S(2)}, u32[]{:S(2)}) async-start(f32[16,32,128]{2,1,0:T(8,128)} %broadcast_in_dim.16), calls=%async_computation.3 | async-start | bytes 524288 | tf_op jit(solution)/shard_map/all_to_all | solution.py:362
  128.2 8.1 %collective-permute-start.12 = (bf16[2,256,128]{2,1,0:T(8,128)(2,1)S(1)}, bf16[2,256,128]{2,1,0:T(8,128)(2,1)S(1)}, u32[]{:S(2)}, u32[]{:S(2)}) collective-permute-start(bf16[2,256,128]{2,1,0:T(8,128)(2,1)S(1)} %get-tuple-element.38), channel_id=1, source_target_pairs={{0,32},{16,48},{32,64},{48,80},{64,96},{80,112},{96,0},{112,16},{1... | collective-permute-start | bytes 393224 | tf_op jit(solution)/shard_map/ppermute | solution.py:368
  128.3 8.1 %collective-permute-start.13 = (bf16[2,256,128]{2,1,0:T(8,128)(2,1)S(1)}, bf16[2,256,128]{2,1,0:T(8,128)(2,1)S(1)}, u32[]{:S(2)}, u32[]{:S(2)}) collective-permute-start(bf16[2,256,128]{2,1,0:T(8,128)(2,1)S(1)} %get-tuple-element.39), channel_id=1, source_target_pairs={{0,64},{16,80},{32,96},{48,112},{64,0},{80,16},{96,32},{112,48},{1... | collective-permute-start | bytes 393224 | tf_op jit(solution)/shard_map/ppermute | solution.py:368
  131.1 5.9 %collective-permute-start.14 = (bf16[2,256,128]{2,1,0:T(8,128)(2,1)S(1)}, bf16[2,256,128]{2,1,0:T(8,128)(2,1)S(1)}, u32[]{:S(2)}, u32[]{:S(2)}) collective-permute-start(bf16[2,256,128]{2,1,0:T(8,128)(2,1)S(1)} %get-tuple-element.40), channel_id=1, source_target_pairs={{0,96},{16,112},{32,0},{48,16},{64,32},{80,48},{96,64},{112,80},{1... | collective-permute-start | bytes 393224 | tf_op jit(solution)/shard_map/ppermute | solution.py:368

commit v3 on v2

--- a/solution.py
+++ b/solution.py
@@ -21,17 +21,25 @@
 
 def cell_lists(out_block, slot, out_blocks, slots):
     count = out_block.shape[0]
+    cells = out_blocks * slots
     ids = jnp.arange(count, dtype=jnp.int32)
     cell = out_block * slots + slot
     order = cell * count + ids
     place = jnp.sum((order[None, :] < order[:, None]).astype(jnp.int32), axis=1)
     members = jnp.sum(jnp.where(place[None, :] == ids[:, None], ids[None, :], 0), axis=1)
-    edges = jnp.arange(out_blocks * slots + 1, dtype=jnp.int32)
+    edges = jnp.arange(cells + 1, dtype=jnp.int32)
     starts = jnp.sum((cell[None, :] < edges[:, None]).astype(jnp.int32), axis=1)
-    return starts, members
-
-
-def densify_kernel(starts, members, a_hbm, *refs, out_blocks, slots, core):
+    earlier = (cell[None, :] == cell[:, None]) & (ids[None, :] < ids[:, None])
+    target = jnp.where(jnp.any(earlier, axis=1), cells, cell)
+    several = (starts[1:] - starts[:-1] > 1).astype(jnp.int32)
+    ahead = jnp.sum(jnp.where(edges[None, :-1] < edges[:, None], several[None, :], 0), axis=1)
+    turn = jnp.where(several > 0, ahead[:-1], -1)
+    at = jnp.arange(count // 2, dtype=jnp.int32)
+    shared = jnp.sum(jnp.where(turn[None, :] == at[:, None], edges[None, :-1], 0), axis=1)
+    return target, members, starts, shared, ahead[:: slots]
+
+
+def densify_kernel(target, members, starts, shared, ends, a_hbm, *refs, out_blocks, slots, core):
     d_hbm, a_buf, d_buf, in_sem, out_sem = refs[-5:]
     count, size, _ = a_hbm.shape
     chunks = in_sem.shape[0]
@@ -45,26 +53,50 @@
         rows = block(o, size)
         return pltpu.make_async_copy(d_buf.at[rows], d_hbm.at[rows], out_sem.at[o])
 
+    def store(cell, values):
+        d_buf[block(cell // slots, size), block(cell % slots, size)] = values
+
     @pl.when(lax.axis_index("row") % 2 == core)
     def _():
         for i in range(chunks):
             fetch(i).start()
-        for i in range(chunks):
+
+        def clear(o, _):
+            d_buf[block(o, size), :] = jnp.zeros((size, slots * size), jnp.bfloat16)
+            return 0
+
+        lax.fori_loop(0, out_blocks, clear, 0)
+
+        def lay(i, _):
             fetch(i).wait()
 
+            def eight(j, _):
+                for q in range(8):
+                    k = i * step + j * 8 + q
+                    store(target[k], a_buf[k])
+                return 0
+
+            lax.fori_loop(0, step // 8, eight, 0)
+            return 0
+
+        lax.fori_loop(0, chunks, lay, 0)
+
         def one_row(o, _):
-            def one_cell(t, _):
-                at = o * slots + t
+            def one_cell(j, _):
+                cell = shared[j]
+                first = starts[cell]
+                total = a_buf[members[first]].astype(jnp.float32)
+                total = total + a_buf[members[first + 1]].astype(jnp.float32)
                 total = lax.fori_loop(
-                    starts[at],
-                    starts[at + 1],
+                    first + 2,
+                    starts[cell + 1],
                     lambda k, s: s + a_buf[members[k]].astype(jnp.float32),
-                    jnp.zeros((size, size), jnp.float32),
+                    total,
                 )
-                d_buf[block(o, size), block(t, size)] = total.astype(jnp.bfloat16)
+                store(cell, total.astype(jnp.bfloat16))
                 return 0
 
-            lax.fori_loop(0, slots, one_cell, 0)
+            lax.fori_loop(ends[o], ends[o + 1], one_cell, 0)
             put(o).start()
             return 0
 
@@ -73,25 +105,25 @@
             put(o).wait()
 
 
-def densify(starts, members, edges, out_blocks, slots, core, before=()):
+def densify(lists, edges, out_blocks, slots, core, before=()):
     count, size, _ = edges.shape
     shape = (out_blocks * size, slots * size)
     return pl.pallas_call(
         functools.partial(densify_kernel, out_blocks=out_blocks, slots=slots, core=core),
         out_shape=jax.ShapeDtypeStruct(shape, jnp.bfloat16),
-        in_specs=[SMEM, SMEM, ANY] + [ANY] * len(before),
+        in_specs=[SMEM] * len(lists) + [ANY] * (1 + len(before)),
         out_specs=ANY,
-        input_output_aliases={3 + i: i for i in range(len(before))},
+        input_output_aliases={len(lists) + 1 + i: i for i in range(len(before))},
         scratch_shapes=[
             pltpu.VMEM(edges.shape, jnp.bfloat16),
-            pltpu.VMEM(shape, jnp.bfloat16),
+            pltpu.VMEM((shape[0] + size, shape[1]), jnp.bfloat16),
             pltpu.SemaphoreType.DMA((math.gcd(count, 16),)),
             pltpu.SemaphoreType.DMA((out_blocks,)),
         ],
         compiler_params=pltpu.CompilerParams(vmem_limit_bytes=40 << 20),
         cost_estimate=pl.CostEstimate(flops=0, bytes_accessed=4 * edges.size, transcendentals=0),
         name="densify",
-    )(starts, members, edges, *before)
+    )(*lists, edges, *before)
 
 
 def block_place(wanted, row, chips, panels, ahead):
@@ -230,7 +262,7 @@
     rows, cols = dense.shape
     width = weight.shape[0]
     sent_rows = cols // size // peers * width + width // peers * (width // size)
-    row_step, col_step = 4 * size, 4 * size
+    row_step, col_step = 4 * size, 8 * size
     grads = jax.ShapeDtypeStruct((peers, sent_rows, size), jnp.bfloat16)
     return pl.pallas_call(
         layer_kernel,
@@ -371,17 +403,17 @@
 
     incoming = exchange(wanted, "col")
     mine = [features] + [to_chip_ahead(features, d) for d in range(1, chips)]
-    incoming, *mine = lax.optimization_barrier((incoming, *mine))
+    incoming, mine[2] = lax.optimization_barrier((incoming, mine[2]))
     pieces = mine + [to_other_core(piece) for piece in mine]
     sends = pick_blocks(incoming, pieces)
 
     coords = block_coords[0, 0]
-    starts, members = cell_lists(coords[:, 0], coords[:, 1], out_blocks, slots)
+    lists = cell_lists(coords[:, 0], coords[:, 1], out_blocks, slots)
     edges = adjacency[0, 0]
-    dense = densify(starts, members, edges, out_blocks, slots, 1)
+    dense = densify(lists, edges, out_blocks, slots, 1)
     sends, dense = lax.optimization_barrier((sends, dense))
     table = exchange(sends, "col").reshape(slots * size, width)
-    dense = densify(starts, members, edges, out_blocks, slots, 0, (dense,))
+    dense = densify(lists, edges, out_blocks, slots, 0, (dense,))
 
     activations, grads = layer(dense, table, weight, cotangent, size, grid_cols)
 
@@ -396,11 +428,12 @@
     own, *messages = chip_sums(keep, to_other_core(send), chips)
     strip, *messages = lax.optimization_barrier((strip, *messages))
     parts = [to_chip_ahead(message, d + 1) for d, message in enumerate(messages)]
+
+    copies = jnp.broadcast_to(strip.astype(jnp.bfloat16)[None], (grid_cols, *strip.shape))
+    strips = exchange(copies, "col").reshape(grid_cols, width // size, width // grid_cols, size)
+    weight_grad = jnp.swapaxes(strips, 1, 2).reshape(width, width).astype(jnp.float32)
+    own, weight_grad = lax.optimization_barrier((own, weight_grad))
     feature_grad = owner_sum(own, parts)
-
-    copies = jnp.broadcast_to(strip[None], (grid_cols, *strip.shape))
-    strips = exchange(copies, "col").reshape(grid_cols, width // size, width // grid_cols, size)
-    weight_grad = jnp.swapaxes(strips, 1, 2).reshape(width, width)
     return (activations, weight_grad, feature_grad)
 
 

time: 139 us -> 130 us (0.935)
  Pallas kernels: 46.6 us -> 40.1 us
  blocking collectives: 26.4 us -> 22.3 us
    all_to_all x3, waiting for transfers between devices: 6.46 us -> 13.8 us  [exchange(): return lax.all_to_all(values, axis, split_axis=0, concat_axis=0, tiled=True)]
    ppermute x9, waiting for transfers between devices: 10.7 us -> 3.57 us  [to_chip_ahead(): lax.ppermute(values, 'row', [(r, (r + 2 * ahead) % grid_rows) for r in ra...]
    pallas_call x2, Pallas kernels: 23.1 us -> 17.3 us  [densify(): pl.pallas_call(functools.partial(densify_kernel, out_blocks=out_blocks, s...]
    all_to_all x1, blocking collectives: 26.4 us -> 22.3 us  [exchange(): return lax.all_to_all(values, axis, split_axis=0, concat_axis=0, tiled=True)]
    ppermute x9, starting transfers between devices: 11.8 us -> 13.4 us  [to_chip_ahead(): lax.ppermute(values, 'row', [(r, (r + 2 * ahead) % grid_rows) for r in ra...]
  transfers between devices with their start and end apart: 18 -> 18, of which waited for: 7 -> 6; matrix products, arithmetic and copies ran while one was open for 2% -> 4% of each run, Pallas kernels for 17% -> 13%
where the time goes in v3:
time: 130 us
  starting transfers between devices  42.2 us (32%)
  Pallas kernels  40.1 us (31%)
  blocking collectives  22.3 us (17%)
  waiting for transfers between devices  18.8 us (14%)
  local copies, waits for them, and re-layouts  3.17 us (2%)
  other arithmetic  2.22 us (2%)
    all_to_all x1, blocking collectives, exchange(): return lax.all_to_all(values, axis, split_axis=0, concat_axis=0, tiled=True)  22.3 us
    pallas_call x2, Pallas kernels, densify(): pl.pallas_call(functools.partial(densify_kernel, out_blocks=out_blocks, s...  17.3 us
    pallas_call x1, Pallas kernels, layer(): pl.pallas_call(layer_kernel, out_shape=(jax.ShapeDtypeStruct(cotangent.sh...  16.1 us
    all_to_all x3, starting transfers between devices, exchange(): return lax.all_to_all(values, axis, split_axis=0, concat_axis=0, tiled=True)  15.3 us
    all_to_all x3, waiting for transfers between devices, exchange(): return lax.all_to_all(values, axis, split_axis=0, concat_axis=0, tiled=True)  13.8 us
    ppermute x6, starting transfers between devices, to_other_core(): return lax.ppermute(values, 'row', [(r, r ^ 1) for r in range(grid_rows)])  13.5 us
    ppermute x9, starting transfers between devices, to_chip_ahead(): lax.ppermute(values, 'row', [(r, (r + 2 * ahead) % grid_rows) for r in ra...  13.4 us
    pallas_call x1, Pallas kernels, pick_blocks(): pl.pallas_call(pick_kernel, out_shape=jax.ShapeDtypeStruct((picks, size,...  3.75 us
  transfers between devices with their start and end apart: 18, of which 6 were waited for; matrix products, arithmetic and copies ran while one was open for 4% of the time, Pallas kernels for 13%

profile of v3, /device:TPU:0, one launch (start us, length us, event | category | flops | bytes accessed | tf_op | source)
XLA Modules:
  0.0 129.7 jit_solution(3923037589563646003)
XLA Ops:
  0.6 2.9 %collective-permute-start.2 = (bf16[2,128,256]{2,1,0:T(8,128)(2,1)}, bf16[2,128,256]{2,1,0:T(8,128)(2,1)S(1)}, u32[]{:S(2)}, u32[]{:S(2)}) collective-permute-start(bf16[2,128,256]{2,1,0:T(8,128)(2,1)} %refs_0_.1), channel_id=1, source_target_pairs={{0,96},{16,112},{32,0},{48,16},{64,32},{80,48},{96,64},{112,80},{1... | collective-permute-start | bytes 393224 | tf_op jit(solution)/shard_map/ppermute | solution.py:400
  3.5 0.0 collective-permute-start.1
  3.5 2.3 %collective-permute-start = (bf16[2,128,256]{2,1,0:T(8,128)(2,1)}, bf16[2,128,256]{2,1,0:T(8,128)(2,1)S(1)}, u32[]{:S(2)}, u32[]{:S(2)}) collective-permute-start(bf16[2,128,256]{2,1,0:T(8,128)(2,1)} %refs_0_.1), channel_id=1, source_target_pairs={{0,64},{16,80},{32,96},{48,112},{64,0},{80,16},{96,32},{112,48},{1... | collective-permute-start | bytes 393224 | tf_op jit(solution)/shard_map/ppermute | solution.py:400
  5.8 0.0 collective-permute-start.3
  5.8 1.4 %copy.22 = s32[16,1,2]{2,1,0:T(1,128)} copy(s32[16,1,2]{0,2,1:T(2,128)} %bitcast.28) | data formatting | bytes 256 | tf_op jit(solution)/shard_map/all_to_all | solution.py:394
  7.2 8.0 %all-to-all-start = ((s32[16,1,2]{2,1,0:T(1,128)}), s32[16,1,2]{2,1,0:T(1,128)S(1)}, u32[]{:S(2)}, u32[]{:S(2)}) async-start(s32[16,1,2]{2,1,0:T(1,128)} %copy.22), calls=%async_computation | async-start | bytes 16384 | tf_op jit(solution)/shard_map/all_to_all | solution.py:394
  15.2 0.8 iota_add_fusion
  16.0 0.2 fusion.1
  16.3 0.2 convert_reduce_fusion.starts
  16.5 0.1 fusion.2
  16.6 0.2 select_reduce_fusion
  16.8 0.1 slice_select_fusion
  16.9 0.2 convert_reduce_fusion.1
  17.1 5.6 %all-to-all-done = s32[16,1,2]{2,1,0:T(1,128)S(1)} async-done(((s32[16,1,2]{2,1,0:T(1,128)}), s32[16,1,2]{2,1,0:T(1,128)S(1)}, u32[]{:S(2)}, u32[]{:S(2)}) %all-to-all-start) | async-done | bytes 160 | tf_op jit(solution)/shard_map/all_to_all | solution.py:394
  22.7 0.1 copy.23
  22.8 0.0 collective-permute-done.refs_2_
  22.8 0.0 collective-permute-start.5
  22.8 0.0 collective-permute-done.2.refs_3_
  22.8 0.5 collective-permute-start.6
  23.3 0.0 collective-permute-done.1.refs_1_
  23.3 0.1 collective-permute-start.4
  23.4 0.2 select_reduce_fusion.1.members
  23.6 0.1 slice.33.ends
  23.7 0.1 select_reduce_fusion.2.shared
  23.9 0.0 copy-start
  23.9 1.0 densify.2.refs_0_
  24.8 0.1 copy.24.incoming
  24.9 0.0 collective-permute-done.3.refs_4_
  24.9 0.0 collective-permute-done.6.refs_7_
  24.9 0.0 collective-permute-done.4.refs_5_
  24.9 0.0 collective-permute-done.5.refs_6_
  25.0 3.8 %pick_blocks.1 = bf16[32,128,256]{2,1,0:T(8,128)(2,1)} custom-call(s32[16,2]{1,0:T(8,128)S(1)} %copy.24.incoming, bf16[2,128,256]{2,1,0:T(8,128)(2,1)S(1)} %copy-done, bf16[2,128,256]{2,1,0:T(8,128)(2,1)S(1)} %collective-permute-done.1.refs_1_, bf16[2,128,256]{2,1,0:T(8,128)(2,1)S(1)} %collective-permute-done.refs_2_, ...), custom_call_target="tpu_custom_call" | custom-call | bytes 4194304 | tf_op jit(solution)/shard_map/pick_blocks/pallas_call | solution.py:163
  28.7 3.7 %all-to-all-start.1 = ((bf16[32,128,256]{2,1,0:T(8,128)(2,1)}), bf16[32,128,256]{2,1,0:T(8,128)(2,1)S(1)}, u32[]{:S(2)}, u32[]{:S(2)}) async-start(bf16[32,128,256]{2,1,0:T(8,128)(2,1)} %pick_blocks.1), calls=%async_computation.1 | async-start | bytes 4194304 | tf_op jit(solution)/shard_map/all_to_all | solution.py:394
  32.5 0.0 copy-start.1
  32.5 0.0 copy-start.2
  32.5 16.3 %densify.3.dense = bf16[2048,4096]{1,0:T(8,128)(2,1)} custom-call(s32[512]{0:T(512)S(1)} %get-tuple-element.42.target, s32[512]{0:T(512)S(1)} %select_reduce_fusion.1.members, s32[513]{0:T(1024)S(1)} %convert_reduce_fusion.starts, s32[256]{0:T(256)S(1)} %select_reduce_fusion.2.shared, s32[17]{0:T(128)S(1)} %slice.33.ends, ...), custom_call_target="tpu_custom_call", output_to_operand_aliasing={{}: (6, {})} | custom-call | bytes 33554432 | tf_op jit(solution)/shard_map/densify/pallas_call | solution.py:111
  48.8 4.7 %all-to-all-done.1 = bf16[32,128,256]{2,1,0:T(8,128)(2,1)S(1)} async-done(((bf16[32,128,256]{2,1,0:T(8,128)(2,1)}), bf16[32,128,256]{2,1,0:T(8,128)(2,1)S(1)}, u32[]{:S(2)}, u32[]{:S(2)}) %all-to-all-start.1) | async-done | bytes 2097184 | tf_op jit(solution)/shard_map/all_to_all | solution.py:394
  53.5 0.0 copy-done.1
  53.5 16.1 %layer.1 = (bf16[2048,256]{1,0:T(8,128)(2,1)}, bf16[16,544,128]{2,1,0:T(8,128)(2,1)S(1)}) custom-call(bf16[2048,4096]{1,0:T(8,128)(2,1)} %densify.3.dense, bf16[4096,256]{1,0:T(8,128)(2,1)S(1)} %bitcast.16, bf16[256,256]{1,0:T(8,128)(2,1)S(1)} %copy-done.2, bf16[2048,256]{1,0:T(8,128)(2,1)S(1)} %copy-done.1), custom_call_target="tpu_custom_call" | custom-call | flops 8589934592 | bytes 16777216 | tf_op jit(solution)/shard_map/layer/pallas_call | solution.py:267
  69.7 22.3 %all_to_all.27.returned = bf16[16,544,128]{2,1,0:T(8,128)(2,1)S(1)} all-to-all(bf16[16,544,128]{2,1,0:T(8,128)(2,1)S(1)} %get-tuple-element.26), channel_id=1, replica_groups=mesh['row'=8,'col'=16] {'col'}, dimensions={0} | all-to-all | bytes 4456448 | tf_op jit(solution)/shard_map/all_to_all | solution.py:394
  92.0 2.0 %group_sums.1 = (f32[8,256,128]{2,1,0:T(8,128)S(1)}, bf16[8,256,128]{2,1,0:T(8,128)(2,1)S(1)}) custom-call(s32[16,2]{1,0:T(8,128)S(1)} %copy.24.incoming, bf16[16,544,128]{2,1,0:T(8,128)(2,1)S(1)} %all_to_all.27.returned), custom_call_target="tpu_custom_call" | custom-call | flops 1114112 | bytes 4456448 | tf_op jit(solution)/shard_map/group_sums/pallas_call | solution.py:316
  94.0 12.8 %collective-permute-start.7 = (bf16[8,256,128]{2,1,0:T(8,128)(2,1)S(1)}, bf16[8,256,128]{2,1,0:T(8,128)(2,1)S(1)}, u32[]{:S(2)}, u32[]{:S(2)}) collective-permute-start(bf16[8,256,128]{2,1,0:T(8,128)(2,1)S(1)} %get-tuple-element.28), channel_id=1, source_target_pairs={{0,16},{16,0},{32,48},{48,32},{64,80},{80,64},{96,112},{112,96},{1... | collective-permute-start | bytes 1572872 | tf_op jit(solution)/shard_map/ppermute | solution.py:397
  106.9 0.1 collective-permute-start.8
  107.0 1.4 %collective-permute-done.8 = f32[32,128]{1,0:T(8,128)S(1)} collective-permute-done((f32[32,128]{1,0:T(8,128)S(1)}, f32[32,128]{1,0:T(8,128)S(1)}, u32[]{:S(2)}, u32[]{:S(2)}) %collective-permute-start.8) | collective-permute-done | bytes 16416 | tf_op jit(solution)/shard_map/ppermute | solution.py:397
  108.4 1.1 collective-permute-start.11
  109.5 0.9 collective-permute-start.10
  110.4 1.7 %collective-permute-start.9 = (f32[32,128]{1,0:T(8,128)S(1)}, f32[32,128]{1,0:T(8,128)S(1)}, u32[]{:S(2)}, u32[]{:S(2)}) collective-permute-start(f32[32,128]{1,0:T(8,128)S(1)} %add.41), channel_id=1, source_target_pairs={{0,64},{16,80},{32,96},{48,112},{64,0},{80,16},{96,32},{112,48},{1... | collective-permute-start | bytes 49160 | tf_op jit(solution)/shard_map/ppermute | solution.py:400
  112.1 0.0 collective-permute-done.11
  112.1 2.5 %collective-permute-done.10 = f32[32,128]{1,0:T(8,128)S(1)} collective-permute-done((f32[32,128]{1,0:T(8,128)S(1)}, f32[32,128]{1,0:T(8,128)S(1)}, u32[]{:S(2)}, u32[]{:S(2)}) %collective-permute-start.10) | collective-permute-done | bytes 16416 | tf_op jit(solution)/shard_map/ppermute | solution.py:400
  114.7 1.0 collective-permute-done.9
  115.7 0.0 collective-permute-done.7.arrived
  115.7 0.1 chip_sums.1
  115.8 0.7 broadcast_in_dim.75
  116.5 3.5 %all-to-all-start.3 = ((bf16[16,32,128]{2,1,0:T(8,128)(2,1)}), bf16[16,32,128]{2,1,0:T(8,128)(2,1)S(1)}, u32[]{:S(2)}, u32[]{:S(2)}) async-start(bf16[16,32,128]{2,1,0:T(8,128)(2,1)} %broadcast_in_dim.75), calls=%async_computation.3 | async-start | bytes 262144 | tf_op jit(solution)/shard_map/all_to_all | solution.py:394
  120.0 1.7 %collective-permute-start.12 = (bf16[2,256,128]{2,1,0:T(8,128)(2,1)S(1)}, bf16[2,256,128]{2,1,0:T(8,128)(2,1)S(1)}, u32[]{:S(2)}, u32[]{:S(2)}) collective-permute-start(bf16[2,256,128]{2,1,0:T(8,128)(2,1)S(1)} %get-tuple-element.36), channel_id=1, source_target_pairs={{0,32},{16,48},{32,64},{48,80},{64,96},{80,112},{96,0},{112,16},{1... | collective-permute-start | bytes 393224 | tf_op jit(solution)/shard_map/ppermute | solution.py:400
  121.7 2.2 %collective-permute-start.13 = (bf16[2,256,128]{2,1,0:T(8,128)(2,1)S(1)}, bf16[2,256,128]{2,1,0:T(8,128)(2,1)S(1)}, u32[]{:S(2)}, u32[]{:S(2)}) collective-permute-start(bf16[2,256,128]{2,1,0:T(8,128)(2,1)S(1)} %get-tuple-element.37), channel_id=1, source_target_pairs={{0,64},{16,80},{32,96},{48,112},{64,0},{80,16},{96,32},{112,48},{1... | collective-permute-start | bytes 393224 | tf_op jit(solution)/shard_map/ppermute | solution.py:400
  123.9 0.6 collective-permute-start.14
  124.5 3.5 %all-to-all-done.3 = bf16[16,32,128]{2,1,0:T(8,128)(2,1)S(1)} async-done(((bf16[16,32,128]{2,1,0:T(8,128)(2,1)}), bf16[16,32,128]{2,1,0:T(8,128)(2,1)S(1)}, u32[]{:S(2)}, u32[]{:S(2)}) %all-to-all-start.3) | async-done | bytes 131104 | tf_op jit(solution)/shard_map/all_to_all | solution.py:394
  128.0 0.1 copy.26
  128.1 0.7 copy.29
  128.9 0.0 collective-permute-done.12.refs_0_
  128.9 0.0 collective-permute-done.13.refs_1_
  128.9 0.0 collective-permute-done.14.refs_2_
  128.9 0.8 owner_sum.1
  (9 shorter events, 0.1 us)
Async XLA Ops:
  0.6 22.2 %collective-permute-start.2 = (bf16[2,128,256]{2,1,0:T(8,128)(2,1)}, bf16[2,128,256]{2,1,0:T(8,128)(2,1)S(1)}, u32[]{:S(2)}, u32[]{:S(2)}) collective-permute-start(bf16[2,128,256]{2,1,0:T(8,128)(2,1)} %refs_0_.1), channel_id=1, source_target_pairs={{0,96},{16,112},{32,0},{48,16},{64,32},{80,48},{96,64},{112,80},{1... | collective-permute-start | bytes 393224 | tf_op jit(solution)/shard_map/ppermute | solution.py:400
  3.5 19.8 %collective-permute-start.1 = (bf16[2,128,256]{2,1,0:T(8,128)(2,1)}, bf16[2,128,256]{2,1,0:T(8,128)(2,1)S(1)}, u32[]{:S(2)}, u32[]{:S(2)}) collective-permute-start(bf16[2,128,256]{2,1,0:T(8,128)(2,1)} %refs_0_.1), channel_id=1, source_target_pairs={{0,32},{16,48},{32,64},{48,80},{64,96},{80,112},{96,0},{112,16},{1... | collective-permute-start | bytes 393224 | tf_op jit(solution)/shard_map/ppermute | solution.py:400
  3.5 19.3 %collective-permute-start = (bf16[2,128,256]{2,1,0:T(8,128)(2,1)}, bf16[2,128,256]{2,1,0:T(8,128)(2,1)S(1)}, u32[]{:S(2)}, u32[]{:S(2)}) collective-permute-start(bf16[2,128,256]{2,1,0:T(8,128)(2,1)} %refs_0_.1), channel_id=1, source_target_pairs={{0,64},{16,80},{32,96},{48,112},{64,0},{80,16},{96,32},{112,48},{1... | collective-permute-start | bytes 393224 | tf_op jit(solution)/shard_map/ppermute | solution.py:400
  5.8 19.1 %collective-permute-start.3 = (bf16[2,128,256]{2,1,0:T(8,128)(2,1)}, bf16[2,128,256]{2,1,0:T(8,128)(2,1)S(1)}, u32[]{:S(2)}, u32[]{:S(2)}) collective-permute-start(bf16[2,128,256]{2,1,0:T(8,128)(2,1)} %refs_0_.1), channel_id=1, source_target_pairs={{0,16},{16,0},{32,48},{48,32},{64,80},{80,64},{96,112},{112,96},{1... | collective-permute-start | bytes 393224 | tf_op jit(solution)/shard_map/ppermute | solution.py:397
  7.2 15.5 %all-to-all-start = ((s32[16,1,2]{2,1,0:T(1,128)}), s32[16,1,2]{2,1,0:T(1,128)S(1)}, u32[]{:S(2)}, u32[]{:S(2)}) async-start(s32[16,1,2]{2,1,0:T(1,128)} %copy.22), calls=%async_computation | async-start | bytes 16384 | tf_op jit(solution)/shard_map/all_to_all | solution.py:394
  22.8 2.1 %collective-permute-start.5 = (bf16[2,128,256]{2,1,0:T(8,128)(2,1)S(1)}, bf16[2,128,256]{2,1,0:T(8,128)(2,1)S(1)}, u32[]{:S(2)}, u32[]{:S(2)}) collective-permute-start(bf16[2,128,256]{2,1,0:T(8,128)(2,1)S(1)} %collective-permute-done.refs_2_), channel_id=1, source_target_pairs={{0,16},{16,0},{32,48},{48,32},{64,80},{80,64},{96,112},{112,96},{1... | collective-permute-start | bytes 393224 | tf_op jit(solution)/shard_map/ppermute | solution.py:397
  22.8 2.1 %collective-permute-start.6 = (bf16[2,128,256]{2,1,0:T(8,128)(2,1)S(1)}, bf16[2,128,256]{2,1,0:T(8,128)(2,1)S(1)}, u32[]{:S(2)}, u32[]{:S(2)}) collective-permute-start(bf16[2,128,256]{2,1,0:T(8,128)(2,1)S(1)} %collective-permute-done.2.refs_3_), channel_id=1, source_target_pairs={{0,16},{16,0},{32,48},{48,32},{64,80},{80,64},{96,112},{112,96},{1... | collective-permute-start | bytes 393224 | tf_op jit(solution)/shard_map/ppermute | solution.py:397
  23.3 1.6 %collective-permute-start.4 = (bf16[2,128,256]{2,1,0:T(8,128)(2,1)S(1)}, bf16[2,128,256]{2,1,0:T(8,128)(2,1)S(1)}, u32[]{:S(2)}, u32[]{:S(2)}) collective-permute-start(bf16[2,128,256]{2,1,0:T(8,128)(2,1)S(1)} %collective-permute-done.1.refs_1_), channel_id=1, source_target_pairs={{0,16},{16,0},{32,48},{48,32},{64,80},{80,64},{96,112},{112,96},{1... | collective-permute-start | bytes 393224 | tf_op jit(solution)/shard_map/ppermute | solution.py:397
  23.9 1.1 copy-start
  28.7 24.8 %all-to-all-start.1 = ((bf16[32,128,256]{2,1,0:T(8,128)(2,1)}), bf16[32,128,256]{2,1,0:T(8,128)(2,1)S(1)}, u32[]{:S(2)}, u32[]{:S(2)}) async-start(bf16[32,128,256]{2,1,0:T(8,128)(2,1)} %pick_blocks.1), calls=%async_computation.1 | async-start | bytes 4194304 | tf_op jit(solution)/shard_map/all_to_all | solution.py:394
  32.5 21.0 %copy-start.1 = (bf16[2048,256]{1,0:T(8,128)(2,1)S(1)}, bf16[2048,256]{1,0:T(8,128)(2,1)}, u32[]{:S(2)}) copy-start(bf16[2048,256]{1,0:T(8,128)(2,1)} %cotangent.1) | copy-start | bytes 3145732
  32.5 21.0 %copy-start.2 = (bf16[256,256]{1,0:T(8,128)(2,1)S(1)}, bf16[256,256]{1,0:T(8,128)(2,1)}, u32[]{:S(2)}) copy-start(bf16[256,256]{1,0:T(8,128)(2,1)} %weight.1) | copy-start | bytes 393220
  94.0 21.7 %collective-permute-start.7 = (bf16[8,256,128]{2,1,0:T(8,128)(2,1)S(1)}, bf16[8,256,128]{2,1,0:T(8,128)(2,1)S(1)}, u32[]{:S(2)}, u32[]{:S(2)}) collective-permute-start(bf16[8,256,128]{2,1,0:T(8,128)(2,1)S(1)} %get-tuple-element.28), channel_id=1, source_target_pairs={{0,16},{16,0},{32,48},{48,32},{64,80},{80,64},{96,112},{112,96},{1... | collective-permute-start | bytes 1572872 | tf_op jit(solution)/shard_map/ppermute | solution.py:397
  106.9 1.5 %collective-permute-start.8 = (f32[32,128]{1,0:T(8,128)S(1)}, f32[32,128]{1,0:T(8,128)S(1)}, u32[]{:S(2)}, u32[]{:S(2)}) collective-permute-start(f32[32,128]{1,0:T(8,128)S(1)} %convert_reduce_fusion.2), channel_id=1, source_target_pairs={{0,16},{16,0},{32,48},{48,32},{64,80},{80,64},{96,112},{112,96},{1... | collective-permute-start | bytes 49160 | tf_op jit(solution)/shard_map/ppermute | solution.py:397
  108.4 3.8 %collective-permute-start.11 = (f32[32,128]{1,0:T(8,128)S(1)}, f32[32,128]{1,0:T(8,128)S(1)}, u32[]{:S(2)}, u32[]{:S(2)}) collective-permute-start(f32[32,128]{1,0:T(8,128)S(1)} %add.41), channel_id=1, source_target_pairs={{0,96},{16,112},{32,0},{48,16},{64,32},{80,48},{96,64},{112,80},{1... | collective-permute-start | bytes 49160 | tf_op jit(solution)/shard_map/ppermute | solution.py:400
  109.5 5.1 %collective-permute-start.10 = (f32[32,128]{1,0:T(8,128)S(1)}, f32[32,128]{1,0:T(8,128)S(1)}, u32[]{:S(2)}, u32[]{:S(2)}) collective-permute-start(f32[32,128]{1,0:T(8,128)S(1)} %add.41), channel_id=1, source_target_pairs={{0,32},{16,48},{32,64},{48,80},{64,96},{80,112},{96,0},{112,16},{1... | collective-permute-start | bytes 49160 | tf_op jit(solution)/shard_map/ppermute | solution.py:400
  110.4 5.2 %collective-permute-start.9 = (f32[32,128]{1,0:T(8,128)S(1)}, f32[32,128]{1,0:T(8,128)S(1)}, u32[]{:S(2)}, u32[]{:S(2)}) collective-permute-start(f32[32,128]{1,0:T(8,128)S(1)} %add.41), channel_id=1, source_target_pairs={{0,64},{16,80},{32,96},{48,112},{64,0},{80,16},{96,32},{112,48},{1... | collective-permute-start | bytes 49160 | tf_op jit(solution)/shard_map/ppermute | solution.py:400
  116.5 11.5 %all-to-all-start.3 = ((bf16[16,32,128]{2,1,0:T(8,128)(2,1)}), bf16[16,32,128]{2,1,0:T(8,128)(2,1)S(1)}, u32[]{:S(2)}, u32[]{:S(2)}) async-start(bf16[16,32,128]{2,1,0:T(8,128)(2,1)} %broadcast_in_dim.75), calls=%async_computation.3 | async-start | bytes 262144 | tf_op jit(solution)/shard_map/all_to_all | solution.py:394
  120.0 8.8 %collective-permute-start.12 = (bf16[2,256,128]{2,1,0:T(8,128)(2,1)S(1)}, bf16[2,256,128]{2,1,0:T(8,128)(2,1)S(1)}, u32[]{:S(2)}, u32[]{:S(2)}) collective-permute-start(bf16[2,256,128]{2,1,0:T(8,128)(2,1)S(1)} %get-tuple-element.36), channel_id=1, source_target_pairs={{0,32},{16,48},{32,64},{48,80},{64,96},{80,112},{96,0},{112,16},{1... | collective-permute-start | bytes 393224 | tf_op jit(solution)/shard_map/ppermute | solution.py:400
  121.7 7.1 %collective-permute-start.13 = (bf16[2,256,128]{2,1,0:T(8,128)(2,1)S(1)}, bf16[2,256,128]{2,1,0:T(8,128)(2,1)S(1)}, u32[]{:S(2)}, u32[]{:S(2)}) collective-permute-start(bf16[2,256,128]{2,1,0:T(8,128)(2,1)S(1)} %get-tuple-element.37), channel_id=1, source_target_pairs={{0,64},{16,80},{32,96},{48,112},{64,0},{80,16},{96,32},{112,48},{1... | collective-permute-start | bytes 393224 | tf_op jit(solution)/shard_map/ppermute | solution.py:400
  123.9 5.0 %collective-permute-start.14 = (bf16[2,256,128]{2,1,0:T(8,128)(2,1)S(1)}, bf16[2,256,128]{2,1,0:T(8,128)(2,1)S(1)}, u32[]{:S(2)}, u32[]{:S(2)}) collective-permute-start(bf16[2,256,128]{2,1,0:T(8,128)(2,1)S(1)} %get-tuple-element.38), channel_id=1, source_target_pairs={{0,96},{16,112},{32,0},{48,16},{64,32},{80,48},{96,64},{112,80},{1... | collective-permute-start | bytes 393224 | tf_op jit(solution)/shard_map/ppermute | solution.py:400

commit v4 on v3

--- a/solution.py
+++ b/solution.py
@@ -262,7 +262,7 @@
     rows, cols = dense.shape
     width = weight.shape[0]
     sent_rows = cols // size // peers * width + width // peers * (width // size)
-    row_step, col_step = 4 * size, 8 * size
+    row_step, col_step = 4 * size, 16 * size
     grads = jax.ShapeDtypeStruct((peers, sent_rows, size), jnp.bfloat16)
     return pl.pallas_call(
         layer_kernel,

time: 130 us -> 130 us (level)
  transfers between devices with their start and end apart: 18 -> 18, of which waited for: 6 -> 7; matrix products, arithmetic and copies ran while one was open for 4% -> 4% of each run, Pallas kernels for 13% -> 13%
where the time goes in v4:
time: 130 us
  starting transfers between devices  43 us (33%)
  Pallas kernels  39.2 us (30%)
  blocking collectives  22.5 us (17%)
  waiting for transfers between devices  18.7 us (14%)
  local copies, waits for them, and re-layouts  3.17 us (2%)
  other arithmetic  2.22 us (2%)
    all_to_all x1, blocking collectives, exchange(): return lax.all_to_all(values, axis, split_axis=0, concat_axis=0, tiled=True)  22.5 us
    pallas_call x2, Pallas kernels, densify(): pl.pallas_call(functools.partial(densify_kernel, out_blocks=out_blocks, s...  16.9 us
    pallas_call x1, Pallas kernels, layer(): pl.pallas_call(layer_kernel, out_shape=(jax.ShapeDtypeStruct(cotangent.sh...  15.8 us
    all_to_all x3, starting transfers between devices, exchange(): return lax.all_to_all(values, axis, split_axis=0, concat_axis=0, tiled=True)  15.3 us
    ppermute x9, starting transfers between devices, to_chip_ahead(): lax.ppermute(values, 'row', [(r, (r + 2 * ahead) % grid_rows) for r in ra...  14.5 us
    all_to_all x3, waiting for transfers between devices, exchange(): return lax.all_to_all(values, axis, split_axis=0, concat_axis=0, tiled=True)  13.8 us
    ppermute x6, starting transfers between devices, to_other_core(): return lax.ppermute(values, 'row', [(r, r ^ 1) for r in range(grid_rows)])  13.2 us
    pallas_call x1, Pallas kernels, pick_blocks(): pl.pallas_call(pick_kernel, out_shape=jax.ShapeDtypeStruct((picks, size,...  3.75 us
  transfers between devices with their start and end apart: 18, of which 7 were waited for; matrix products, arithmetic and copies ran while one was open for 4% of the time, Pallas kernels for 13%

profile of v4, /device:TPU:0, one launch (start us, length us, event | category | flops | bytes accessed | tf_op | source)
XLA Modules:
  0.0 129.6 jit_solution(10850345034317562178)
XLA Ops:
  0.6 2.9 %collective-permute-start.2 = (bf16[2,128,256]{2,1,0:T(8,128)(2,1)}, bf16[2,128,256]{2,1,0:T(8,128)(2,1)S(1)}, u32[]{:S(2)}, u32[]{:S(2)}) collective-permute-start(bf16[2,128,256]{2,1,0:T(8,128)(2,1)} %refs_0_.1), channel_id=1, source_target_pairs={{0,96},{16,112},{32,0},{48,16},{64,32},{80,48},{96,64},{112,80},{1... | collective-permute-start | bytes 393224 | tf_op jit(solution)/shard_map/ppermute | solution.py:400
  3.5 0.0 collective-permute-start.1
  3.5 2.3 %collective-permute-start = (bf16[2,128,256]{2,1,0:T(8,128)(2,1)}, bf16[2,128,256]{2,1,0:T(8,128)(2,1)S(1)}, u32[]{:S(2)}, u32[]{:S(2)}) collective-permute-start(bf16[2,128,256]{2,1,0:T(8,128)(2,1)} %refs_0_.1), channel_id=1, source_target_pairs={{0,64},{16,80},{32,96},{48,112},{64,0},{80,16},{96,32},{112,48},{1... | collective-permute-start | bytes 393224 | tf_op jit(solution)/shard_map/ppermute | solution.py:400
  5.8 0.0 collective-permute-start.3
  5.8 1.4 %copy.22 = s32[16,1,2]{2,1,0:T(1,128)} copy(s32[16,1,2]{0,2,1:T(2,128)} %bitcast.28) | data formatting | bytes 256 | tf_op jit(solution)/shard_map/all_to_all | solution.py:394
  7.2 8.0 %all-to-all-start = ((s32[16,1,2]{2,1,0:T(1,128)}), s32[16,1,2]{2,1,0:T(1,128)S(1)}, u32[]{:S(2)}, u32[]{:S(2)}) async-start(s32[16,1,2]{2,1,0:T(1,128)} %copy.22), calls=%async_computation | async-start | bytes 16384 | tf_op jit(solution)/shard_map/all_to_all | solution.py:394
  15.2 0.8 iota_add_fusion
  16.0 0.2 fusion.1
  16.3 0.2 convert_reduce_fusion.starts
  16.5 0.1 fusion.2
  16.6 0.2 select_reduce_fusion
  16.8 0.1 slice_select_fusion
  16.9 0.2 convert_reduce_fusion.1
  17.1 5.6 %all-to-all-done = s32[16,1,2]{2,1,0:T(1,128)S(1)} async-done(((s32[16,1,2]{2,1,0:T(1,128)}), s32[16,1,2]{2,1,0:T(1,128)S(1)}, u32[]{:S(2)}, u32[]{:S(2)}) %all-to-all-start) | async-done | bytes 160 | tf_op jit(solution)/shard_map/all_to_all | solution.py:394
  22.7 0.1 copy.23
  22.8 0.0 collective-permute-done.refs_2_
  22.8 0.0 collective-permute-start.5
  22.8 0.0 collective-permute-done.2.refs_3_
  22.8 0.5 collective-permute-start.6
  23.3 0.0 collective-permute-done.1.refs_1_
  23.3 0.1 collective-permute-start.4
  23.4 0.2 select_reduce_fusion.1.members
  23.6 0.1 slice.33.ends
  23.7 0.1 select_reduce_fusion.2.shared
  23.9 0.0 copy-start
  23.9 1.0 densify.2.refs_0_
  24.8 0.1 copy.24.incoming
  24.9 0.0 collective-permute-done.3.refs_4_
  24.9 0.0 collective-permute-done.6.refs_7_
  24.9 0.0 collective-permute-done.4.refs_5_
  24.9 0.0 collective-permute-done.5.refs_6_
  25.0 3.8 %pick_blocks.1 = bf16[32,128,256]{2,1,0:T(8,128)(2,1)} custom-call(s32[16,2]{1,0:T(8,128)S(1)} %copy.24.incoming, bf16[2,128,256]{2,1,0:T(8,128)(2,1)S(1)} %copy-done, bf16[2,128,256]{2,1,0:T(8,128)(2,1)S(1)} %collective-permute-done.1.refs_1_, bf16[2,128,256]{2,1,0:T(8,128)(2,1)S(1)} %collective-permute-done.refs_2_, ...), custom_call_target="tpu_custom_call" | custom-call | bytes 4194304 | tf_op jit(solution)/shard_map/pick_blocks/pallas_call | solution.py:163
  28.7 3.7 %all-to-all-start.1 = ((bf16[32,128,256]{2,1,0:T(8,128)(2,1)}), bf16[32,128,256]{2,1,0:T(8,128)(2,1)S(1)}, u32[]{:S(2)}, u32[]{:S(2)}) async-start(bf16[32,128,256]{2,1,0:T(8,128)(2,1)} %pick_blocks.1), calls=%async_computation.1 | async-start | bytes 4194304 | tf_op jit(solution)/shard_map/all_to_all | solution.py:394
  32.5 0.0 copy-start.1
  32.5 0.0 copy-start.2
  32.5 15.9 %densify.3.dense = bf16[2048,4096]{1,0:T(8,128)(2,1)} custom-call(s32[512]{0:T(512)S(1)} %get-tuple-element.42.target, s32[512]{0:T(512)S(1)} %select_reduce_fusion.1.members, s32[513]{0:T(1024)S(1)} %convert_reduce_fusion.starts, s32[256]{0:T(256)S(1)} %select_reduce_fusion.2.shared, s32[17]{0:T(128)S(1)} %slice.33.ends, ...), custom_call_target="tpu_custom_call", output_to_operand_aliasing={{}: (6, {})} | custom-call | bytes 33554432 | tf_op jit(solution)/shard_map/densify/pallas_call | solution.py:111
  48.4 5.1 %all-to-all-done.1 = bf16[32,128,256]{2,1,0:T(8,128)(2,1)S(1)} async-done(((bf16[32,128,256]{2,1,0:T(8,128)(2,1)}), bf16[32,128,256]{2,1,0:T(8,128)(2,1)S(1)}, u32[]{:S(2)}, u32[]{:S(2)}) %all-to-all-start.1) | async-done | bytes 2097184 | tf_op jit(solution)/shard_map/all_to_all | solution.py:394
  53.5 0.0 copy-done.1
  53.5 15.8 %layer.1 = (bf16[2048,256]{1,0:T(8,128)(2,1)}, bf16[16,544,128]{2,1,0:T(8,128)(2,1)S(1)}) custom-call(bf16[2048,4096]{1,0:T(8,128)(2,1)} %densify.3.dense, bf16[4096,256]{1,0:T(8,128)(2,1)S(1)} %bitcast.16, bf16[256,256]{1,0:T(8,128)(2,1)S(1)} %copy-done.2, bf16[2048,256]{1,0:T(8,128)(2,1)S(1)} %copy-done.1), custom_call_target="tpu_custom_call" | custom-call | flops 8589934592 | bytes 16777216 | tf_op jit(solution)/shard_map/layer/pallas_call | solution.py:267
  69.3 22.5 %all_to_all.27.returned = bf16[16,544,128]{2,1,0:T(8,128)(2,1)S(1)} all-to-all(bf16[16,544,128]{2,1,0:T(8,128)(2,1)S(1)} %get-tuple-element.26), channel_id=1, replica_groups=mesh['row'=8,'col'=16] {'col'}, dimensions={0} | all-to-all | bytes 4456448 | tf_op jit(solution)/shard_map/all_to_all | solution.py:394
  91.8 1.9 %group_sums.1 = (f32[8,256,128]{2,1,0:T(8,128)S(1)}, bf16[8,256,128]{2,1,0:T(8,128)(2,1)S(1)}) custom-call(s32[16,2]{1,0:T(8,128)S(1)} %copy.24.incoming, bf16[16,544,128]{2,1,0:T(8,128)(2,1)S(1)} %all_to_all.27.returned), custom_call_target="tpu_custom_call" | custom-call | flops 1114112 | bytes 4456448 | tf_op jit(solution)/shard_map/group_sums/pallas_call | solution.py:316
  93.7 12.5 %collective-permute-start.7 = (bf16[8,256,128]{2,1,0:T(8,128)(2,1)S(1)}, bf16[8,256,128]{2,1,0:T(8,128)(2,1)S(1)}, u32[]{:S(2)}, u32[]{:S(2)}) collective-permute-start(bf16[8,256,128]{2,1,0:T(8,128)(2,1)S(1)} %get-tuple-element.28), channel_id=1, source_target_pairs={{0,16},{16,0},{32,48},{48,32},{64,80},{80,64},{96,112},{112,96},{1... | collective-permute-start | bytes 1572872 | tf_op jit(solution)/shard_map/ppermute | solution.py:397
  106.2 0.1 collective-permute-start.8
  106.3 1.4 %collective-permute-done.8 = f32[32,128]{1,0:T(8,128)S(1)} collective-permute-done((f32[32,128]{1,0:T(8,128)S(1)}, f32[32,128]{1,0:T(8,128)S(1)}, u32[]{:S(2)}, u32[]{:S(2)}) %collective-permute-start.8) | collective-permute-done | bytes 16416 | tf_op jit(solution)/shard_map/ppermute | solution.py:397
  107.8 1.7 %collective-permute-start.11 = (f32[32,128]{1,0:T(8,128)S(1)}, f32[32,128]{1,0:T(8,128)S(1)}, u32[]{:S(2)}, u32[]{:S(2)}) collective-permute-start(f32[32,128]{1,0:T(8,128)S(1)} %add.41), channel_id=1, source_target_pairs={{0,96},{16,112},{32,0},{48,16},{64,32},{80,48},{96,64},{112,80},{1... | collective-permute-start | bytes 49160 | tf_op jit(solution)/shard_map/ppermute | solution.py:400
  109.4 0.7 collective-permute-start.10
  110.2 2.0 %collective-permute-start.9 = (f32[32,128]{1,0:T(8,128)S(1)}, f32[32,128]{1,0:T(8,128)S(1)}, u32[]{:S(2)}, u32[]{:S(2)}) collective-permute-start(f32[32,128]{1,0:T(8,128)S(1)} %add.41), channel_id=1, source_target_pairs={{0,64},{16,80},{32,96},{48,112},{64,0},{80,16},{96,32},{112,48},{1... | collective-permute-start | bytes 49160 | tf_op jit(solution)/shard_map/ppermute | solution.py:400
  112.2 0.0 collective-permute-done.11
  112.2 2.1 %collective-permute-done.10 = f32[32,128]{1,0:T(8,128)S(1)} collective-permute-done((f32[32,128]{1,0:T(8,128)S(1)}, f32[32,128]{1,0:T(8,128)S(1)}, u32[]{:S(2)}, u32[]{:S(2)}) %collective-permute-start.10) | collective-permute-done | bytes 16416 | tf_op jit(solution)/shard_map/ppermute | solution.py:400
  114.4 1.0 collective-permute-done.9
  115.4 0.0 collective-permute-done.7.arrived
  115.5 0.1 chip_sums.1
  115.6 0.7 broadcast_in_dim.75
  116.2 3.5 %all-to-all-start.3 = ((bf16[16,32,128]{2,1,0:T(8,128)(2,1)}), bf16[16,32,128]{2,1,0:T(8,128)(2,1)S(1)}, u32[]{:S(2)}, u32[]{:S(2)}) async-start(bf16[16,32,128]{2,1,0:T(8,128)(2,1)} %broadcast_in_dim.75), calls=%async_computation.3 | async-start | bytes 262144 | tf_op jit(solution)/shard_map/all_to_all | solution.py:394
  119.8 2.1 %collective-permute-start.12 = (bf16[2,256,128]{2,1,0:T(8,128)(2,1)S(1)}, bf16[2,256,128]{2,1,0:T(8,128)(2,1)S(1)}, u32[]{:S(2)}, u32[]{:S(2)}) collective-permute-start(bf16[2,256,128]{2,1,0:T(8,128)(2,1)S(1)} %get-tuple-element.36), channel_id=1, source_target_pairs={{0,32},{16,48},{32,64},{48,80},{64,96},{80,112},{96,0},{112,16},{1... | collective-permute-start | bytes 393224 | tf_op jit(solution)/shard_map/ppermute | solution.py:400
  121.8 1.9 %collective-permute-start.13 = (bf16[2,256,128]{2,1,0:T(8,128)(2,1)S(1)}, bf16[2,256,128]{2,1,0:T(8,128)(2,1)S(1)}, u32[]{:S(2)}, u32[]{:S(2)}) collective-permute-start(bf16[2,256,128]{2,1,0:T(8,128)(2,1)S(1)} %get-tuple-element.37), channel_id=1, source_target_pairs={{0,64},{16,80},{32,96},{48,112},{64,0},{80,16},{96,32},{112,48},{1... | collective-permute-start | bytes 393224 | tf_op jit(solution)/shard_map/ppermute | solution.py:400
  123.8 0.8 collective-permute-start.14
  124.6 3.1 %all-to-all-done.3 = bf16[16,32,128]{2,1,0:T(8,128)(2,1)S(1)} async-done(((bf16[16,32,128]{2,1,0:T(8,128)(2,1)}), bf16[16,32,128]{2,1,0:T(8,128)(2,1)S(1)}, u32[]{:S(2)}, u32[]{:S(2)}) %all-to-all-start.3) | async-done | bytes 131104 | tf_op jit(solution)/shard_map/all_to_all | solution.py:394
  127.7 0.1 copy.26
  127.9 0.7 copy.29
  128.6 0.0 collective-permute-done.12.refs_0_
  128.6 0.0 collective-permute-done.13.refs_1_
  128.6 0.2 collective-permute-done.14.refs_2_
  128.8 0.8 owner_sum.1
  (9 shorter events, 0.1 us)
Async XLA Ops:
  0.6 22.2 %collective-permute-start.2 = (bf16[2,128,256]{2,1,0:T(8,128)(2,1)}, bf16[2,128,256]{2,1,0:T(8,128)(2,1)S(1)}, u32[]{:S(2)}, u32[]{:S(2)}) collective-permute-start(bf16[2,128,256]{2,1,0:T(8,128)(2,1)} %refs_0_.1), channel_id=1, source_target_pairs={{0,96},{16,112},{32,0},{48,16},{64,32},{80,48},{96,64},{112,80},{1... | collective-permute-start | bytes 393224 | tf_op jit(solution)/shard_map/ppermute | solution.py:400
  3.5 19.8 %collective-permute-start.1 = (bf16[2,128,256]{2,1,0:T(8,128)(2,1)}, bf16[2,128,256]{2,1,0:T(8,128)(2,1)S(1)}, u32[]{:S(2)}, u32[]{:S(2)}) collective-permute-start(bf16[2,128,256]{2,1,0:T(8,128)(2,1)} %refs_0_.1), channel_id=1, source_target_pairs={{0,32},{16,48},{32,64},{48,80},{64,96},{80,112},{96,0},{112,16},{1... | collective-permute-start | bytes 393224 | tf_op jit(solution)/shard_map/ppermute | solution.py:400
  3.5 19.3 %collective-permute-start = (bf16[2,128,256]{2,1,0:T(8,128)(2,1)}, bf16[2,128,256]{2,1,0:T(8,128)(2,1)S(1)}, u32[]{:S(2)}, u32[]{:S(2)}) collective-permute-start(bf16[2,128,256]{2,1,0:T(8,128)(2,1)} %refs_0_.1), channel_id=1, source_target_pairs={{0,64},{16,80},{32,96},{48,112},{64,0},{80,16},{96,32},{112,48},{1... | collective-permute-start | bytes 393224 | tf_op jit(solution)/shard_map/ppermute | solution.py:400
  5.8 19.1 %collective-permute-start.3 = (bf16[2,128,256]{2,1,0:T(8,128)(2,1)}, bf16[2,128,256]{2,1,0:T(8,128)(2,1)S(1)}, u32[]{:S(2)}, u32[]{:S(2)}) collective-permute-start(bf16[2,128,256]{2,1,0:T(8,128)(2,1)} %refs_0_.1), channel_id=1, source_target_pairs={{0,16},{16,0},{32,48},{48,32},{64,80},{80,64},{96,112},{112,96},{1... | collective-permute-start | bytes 393224 | tf_op jit(solution)/shard_map/ppermute | solution.py:397
  7.2 15.5 %all-to-all-start = ((s32[16,1,2]{2,1,0:T(1,128)}), s32[16,1,2]{2,1,0:T(1,128)S(1)}, u32[]{:S(2)}, u32[]{:S(2)}) async-start(s32[16,1,2]{2,1,0:T(1,128)} %copy.22), calls=%async_computation | async-start | bytes 16384 | tf_op jit(solution)/shard_map/all_to_all | solution.py:394
  22.8 2.1 %collective-permute-start.5 = (bf16[2,128,256]{2,1,0:T(8,128)(2,1)S(1)}, bf16[2,128,256]{2,1,0:T(8,128)(2,1)S(1)}, u32[]{:S(2)}, u32[]{:S(2)}) collective-permute-start(bf16[2,128,256]{2,1,0:T(8,128)(2,1)S(1)} %collective-permute-done.refs_2_), channel_id=1, source_target_pairs={{0,16},{16,0},{32,48},{48,32},{64,80},{80,64},{96,112},{112,96},{1... | collective-permute-start | bytes 393224 | tf_op jit(solution)/shard_map/ppermute | solution.py:397
  22.8 2.1 %collective-permute-start.6 = (bf16[2,128,256]{2,1,0:T(8,128)(2,1)S(1)}, bf16[2,128,256]{2,1,0:T(8,128)(2,1)S(1)}, u32[]{:S(2)}, u32[]{:S(2)}) collective-permute-start(bf16[2,128,256]{2,1,0:T(8,128)(2,1)S(1)} %collective-permute-done.2.refs_3_), channel_id=1, source_target_pairs={{0,16},{16,0},{32,48},{48,32},{64,80},{80,64},{96,112},{112,96},{1... | collective-permute-start | bytes 393224 | tf_op jit(solution)/shard_map/ppermute | solution.py:397
  23.3 1.6 %collective-permute-start.4 = (bf16[2,128,256]{2,1,0:T(8,128)(2,1)S(1)}, bf16[2,128,256]{2,1,0:T(8,128)(2,1)S(1)}, u32[]{:S(2)}, u32[]{:S(2)}) collective-permute-start(bf16[2,128,256]{2,1,0:T(8,128)(2,1)S(1)} %collective-permute-done.1.refs_1_), channel_id=1, source_target_pairs={{0,16},{16,0},{32,48},{48,32},{64,80},{80,64},{96,112},{112,96},{1... | collective-permute-start | bytes 393224 | tf_op jit(solution)/shard_map/ppermute | solution.py:397
  23.9 1.1 copy-start
  28.7 24.8 %all-to-all-start.1 = ((bf16[32,128,256]{2,1,0:T(8,128)(2,1)}), bf16[32,128,256]{2,1,0:T(8,128)(2,1)S(1)}, u32[]{:S(2)}, u32[]{:S(2)}) async-start(bf16[32,128,256]{2,1,0:T(8,128)(2,1)} %pick_blocks.1), calls=%async_computation.1 | async-start | bytes 4194304 | tf_op jit(solution)/shard_map/all_to_all | solution.py:394
  32.5 21.0 %copy-start.1 = (bf16[2048,256]{1,0:T(8,128)(2,1)S(1)}, bf16[2048,256]{1,0:T(8,128)(2,1)}, u32[]{:S(2)}) copy-start(bf16[2048,256]{1,0:T(8,128)(2,1)} %cotangent.1) | copy-start | bytes 3145732
  32.5 21.0 %copy-start.2 = (bf16[256,256]{1,0:T(8,128)(2,1)S(1)}, bf16[256,256]{1,0:T(8,128)(2,1)}, u32[]{:S(2)}) copy-start(bf16[256,256]{1,0:T(8,128)(2,1)} %weight.1) | copy-start | bytes 393220
  93.7 21.7 %collective-permute-start.7 = (bf16[8,256,128]{2,1,0:T(8,128)(2,1)S(1)}, bf16[8,256,128]{2,1,0:T(8,128)(2,1)S(1)}, u32[]{:S(2)}, u32[]{:S(2)}) collective-permute-start(bf16[8,256,128]{2,1,0:T(8,128)(2,1)S(1)} %get-tuple-element.28), channel_id=1, source_target_pairs={{0,16},{16,0},{32,48},{48,32},{64,80},{80,64},{96,112},{112,96},{1... | collective-permute-start | bytes 1572872 | tf_op jit(solution)/shard_map/ppermute | solution.py:397
  106.2 1.5 %collective-permute-start.8 = (f32[32,128]{1,0:T(8,128)S(1)}, f32[32,128]{1,0:T(8,128)S(1)}, u32[]{:S(2)}, u32[]{:S(2)}) collective-permute-start(f32[32,128]{1,0:T(8,128)S(1)} %convert_reduce_fusion.2), channel_id=1, source_target_pairs={{0,16},{16,0},{32,48},{48,32},{64,80},{80,64},{96,112},{112,96},{1... | collective-permute-start | bytes 49160 | tf_op jit(solution)/shard_map/ppermute | solution.py:397
  107.8 4.5 %collective-permute-start.11 = (f32[32,128]{1,0:T(8,128)S(1)}, f32[32,128]{1,0:T(8,128)S(1)}, u32[]{:S(2)}, u32[]{:S(2)}) collective-permute-start(f32[32,128]{1,0:T(8,128)S(1)} %add.41), channel_id=1, source_target_pairs={{0,96},{16,112},{32,0},{48,16},{64,32},{80,48},{96,64},{112,80},{1... | collective-permute-start | bytes 49160 | tf_op jit(solution)/shard_map/ppermute | solution.py:400
  109.4 4.9 %collective-permute-start.10 = (f32[32,128]{1,0:T(8,128)S(1)}, f32[32,128]{1,0:T(8,128)S(1)}, u32[]{:S(2)}, u32[]{:S(2)}) collective-permute-start(f32[32,128]{1,0:T(8,128)S(1)} %add.41), channel_id=1, source_target_pairs={{0,32},{16,48},{32,64},{48,80},{64,96},{80,112},{96,0},{112,16},{1... | collective-permute-start | bytes 49160 | tf_op jit(solution)/shard_map/ppermute | solution.py:400
  110.2 5.2 %collective-permute-start.9 = (f32[32,128]{1,0:T(8,128)S(1)}, f32[32,128]{1,0:T(8,128)S(1)}, u32[]{:S(2)}, u32[]{:S(2)}) collective-permute-start(f32[32,128]{1,0:T(8,128)S(1)} %add.41), channel_id=1, source_target_pairs={{0,64},{16,80},{32,96},{48,112},{64,0},{80,16},{96,32},{112,48},{1... | collective-permute-start | bytes 49160 | tf_op jit(solution)/shard_map/ppermute | solution.py:400
  116.2 11.5 %all-to-all-start.3 = ((bf16[16,32,128]{2,1,0:T(8,128)(2,1)}), bf16[16,32,128]{2,1,0:T(8,128)(2,1)S(1)}, u32[]{:S(2)}, u32[]{:S(2)}) async-start(bf16[16,32,128]{2,1,0:T(8,128)(2,1)} %broadcast_in_dim.75), calls=%async_computation.3 | async-start | bytes 262144 | tf_op jit(solution)/shard_map/all_to_all | solution.py:394
  119.8 8.8 %collective-permute-start.12 = (bf16[2,256,128]{2,1,0:T(8,128)(2,1)S(1)}, bf16[2,256,128]{2,1,0:T(8,128)(2,1)S(1)}, u32[]{:S(2)}, u32[]{:S(2)}) collective-permute-start(bf16[2,256,128]{2,1,0:T(8,128)(2,1)S(1)} %get-tuple-element.36), channel_id=1, source_target_pairs={{0,32},{16,48},{32,64},{48,80},{64,96},{80,112},{96,0},{112,16},{1... | collective-permute-start | bytes 393224 | tf_op jit(solution)/shard_map/ppermute | solution.py:400
  121.8 6.8 %collective-permute-start.13 = (bf16[2,256,128]{2,1,0:T(8,128)(2,1)S(1)}, bf16[2,256,128]{2,1,0:T(8,128)(2,1)S(1)}, u32[]{:S(2)}, u32[]{:S(2)}) collective-permute-start(bf16[2,256,128]{2,1,0:T(8,128)(2,1)S(1)} %get-tuple-element.37), channel_id=1, source_target_pairs={{0,64},{16,80},{32,96},{48,112},{64,0},{80,16},{96,32},{112,48},{1... | collective-permute-start | bytes 393224 | tf_op jit(solution)/shard_map/ppermute | solution.py:400
  123.8 5.0 %collective-permute-start.14 = (bf16[2,256,128]{2,1,0:T(8,128)(2,1)S(1)}, bf16[2,256,128]{2,1,0:T(8,128)(2,1)S(1)}, u32[]{:S(2)}, u32[]{:S(2)}) collective-permute-start(bf16[2,256,128]{2,1,0:T(8,128)(2,1)S(1)} %get-tuple-element.38), channel_id=1, source_target_pairs={{0,96},{16,112},{32,0},{48,16},{64,32},{80,48},{96,64},{112,80},{1... | collective-permute-start | bytes 393224 | tf_op jit(solution)/shard_map/ppermute | solution.py:400

commit v5 on v4

--- a/solution.py
+++ b/solution.py
@@ -215,12 +215,11 @@
         w = weight[...]
         pre = jnp.dot(agg, w, preferred_element_type=jnp.float32)
         square = pre * pre
-        tanh = jnp.tanh(GELU_SCALE * (pre + GELU_CUBE * (square * pre)))
-        half = 0.5 * (1.0 + tanh)
+        tanh = jnp.tanh(pre * (GELU_SCALE + (GELU_SCALE * GELU_CUBE) * square))
+        half = 0.5 + 0.5 * tanh
         act_buf[part, :] = (pre * half).astype(jnp.bfloat16)
-        slope = half + (0.5 * GELU_SCALE) * pre * (1.0 - tanh * tanh) * (
-            1.0 + (3 * GELU_CUBE) * square
-        )
+        bend = 0.5 * GELU_SCALE + (1.5 * GELU_SCALE * GELU_CUBE) * square
+        slope = half + (pre - pre * (tanh * tanh)) * bend
         pre_grad = (cotangent[part, :].astype(jnp.float32) * slope).astype(jnp.bfloat16)
         wgrad[...] += lax.dot_general(
             agg, pre_grad, (((0,), (0,)), ((), ())), preferred_element_type=jnp.float32

time: 130 us -> 130 us (level)
  transfers between devices with their start and end apart: 18 -> 18, of which waited for: 7 -> 6; matrix products, arithmetic and copies ran while one was open for 4% -> 4% of each run, Pallas kernels for 13% -> 13%
where the time goes in v5:
time: 130 us; the launch traced here: 129 us
  starting transfers between devices  42.8 us (33%)
  Pallas kernels  39.5 us (30%)
  blocking collectives  22.3 us (17%)
  waiting for transfers between devices  18.5 us (14%)
  local copies, waits for them, and re-layouts  3.17 us (2%)
  other arithmetic  2.22 us (2%)
    all_to_all x1, blocking collectives, exchange(): return lax.all_to_all(values, axis, split_axis=0, concat_axis=0, tiled=True)  22.3 us
    pallas_call x2, Pallas kernels, densify(): pl.pallas_call(functools.partial(densify_kernel, out_blocks=out_blocks, s...  17.3 us
    pallas_call x1, Pallas kernels, layer(): pl.pallas_call(layer_kernel, out_shape=(jax.ShapeDtypeStruct(cotangent.sh...  15.6 us
    all_to_all x3, starting transfers between devices, exchange(): return lax.all_to_all(values, axis, split_axis=0, concat_axis=0, tiled=True)  15.3 us
    ppermute x6, starting transfers between devices, to_other_core(): return lax.ppermute(values, 'row', [(r, r ^ 1) for r in range(grid_rows)])  13.8 us
    ppermute x9, starting transfers between devices, to_chip_ahead(): lax.ppermute(values, 'row', [(r, (r + 2 * ahead) % grid_rows) for r in ra...  13.7 us
    all_to_all x3, waiting for transfers between devices, exchange(): return lax.all_to_all(values, axis, split_axis=0, concat_axis=0, tiled=True)  13.6 us
    pallas_call x1, Pallas kernels, pick_blocks(): pl.pallas_call(pick_kernel, out_shape=jax.ShapeDtypeStruct((picks, size,...  3.75 us
  transfers between devices with their start and end apart: 18, of which 6 were waited for; matrix products, arithmetic and copies ran while one was open for 4% of the time, Pallas kernels for 13%

profile of v5, /device:TPU:0, one launch (start us, length us, event | category | flops | bytes accessed | tf_op | source)
XLA Modules:
  0.0 129.3 jit_solution(11575331441149398816)
XLA Ops:
  0.6 2.9 %collective-permute-start.2 = (bf16[2,128,256]{2,1,0:T(8,128)(2,1)}, bf16[2,128,256]{2,1,0:T(8,128)(2,1)S(1)}, u32[]{:S(2)}, u32[]{:S(2)}) collective-permute-start(bf16[2,128,256]{2,1,0:T(8,128)(2,1)} %refs_0_.1), channel_id=1, source_target_pairs={{0,96},{16,112},{32,0},{48,16},{64,32},{80,48},{96,64},{112,80},{1... | collective-permute-start | bytes 393224 | tf_op jit(solution)/shard_map/ppermute | solution.py:399
  3.5 0.0 collective-permute-start.1
  3.5 2.3 %collective-permute-start = (bf16[2,128,256]{2,1,0:T(8,128)(2,1)}, bf16[2,128,256]{2,1,0:T(8,128)(2,1)S(1)}, u32[]{:S(2)}, u32[]{:S(2)}) collective-permute-start(bf16[2,128,256]{2,1,0:T(8,128)(2,1)} %refs_0_.1), channel_id=1, source_target_pairs={{0,64},{16,80},{32,96},{48,112},{64,0},{80,16},{96,32},{112,48},{1... | collective-permute-start | bytes 393224 | tf_op jit(solution)/shard_map/ppermute | solution.py:399
  5.8 0.0 collective-permute-start.3
  5.8 1.4 %copy.22 = s32[16,1,2]{2,1,0:T(1,128)} copy(s32[16,1,2]{0,2,1:T(2,128)} %bitcast.28) | data formatting | bytes 256 | tf_op jit(solution)/shard_map/all_to_all | solution.py:393
  7.2 8.0 %all-to-all-start = ((s32[16,1,2]{2,1,0:T(1,128)}), s32[16,1,2]{2,1,0:T(1,128)S(1)}, u32[]{:S(2)}, u32[]{:S(2)}) async-start(s32[16,1,2]{2,1,0:T(1,128)} %copy.22), calls=%async_computation | async-start | bytes 16384 | tf_op jit(solution)/shard_map/all_to_all | solution.py:393
  15.2 0.8 iota_add_fusion
  16.0 0.2 fusion.1
  16.3 0.2 convert_reduce_fusion.starts
  16.5 0.1 fusion.2
  16.6 0.2 select_reduce_fusion
  16.8 0.1 slice_select_fusion
  16.9 0.2 convert_reduce_fusion.1
  17.1 5.6 %all-to-all-done = s32[16,1,2]{2,1,0:T(1,128)S(1)} async-done(((s32[16,1,2]{2,1,0:T(1,128)}), s32[16,1,2]{2,1,0:T(1,128)S(1)}, u32[]{:S(2)}, u32[]{:S(2)}) %all-to-all-start) | async-done | bytes 160 | tf_op jit(solution)/shard_map/all_to_all | solution.py:393
  22.7 0.1 copy.23
  22.8 0.0 collective-permute-done.refs_2_
  22.8 0.0 collective-permute-start.5
  22.8 0.0 collective-permute-done.2.refs_3_
  22.8 0.5 collective-permute-start.6
  23.3 0.0 collective-permute-done.1.refs_1_
  23.3 0.1 collective-permute-start.4
  23.4 0.2 select_reduce_fusion.1.members
  23.6 0.1 slice.33.ends
  23.7 0.1 select_reduce_fusion.2.shared
  23.9 0.0 copy-start
  23.9 1.0 densify.2.refs_0_
  24.8 0.1 copy.24.incoming
  24.9 0.0 collective-permute-done.3.refs_4_
  24.9 0.0 collective-permute-done.6.refs_7_
  24.9 0.0 collective-permute-done.4.refs_5_
  24.9 0.0 collective-permute-done.5.refs_6_
  25.0 0.0 copy-done
  25.0 3.8 %pick_blocks.1 = bf16[32,128,256]{2,1,0:T(8,128)(2,1)} custom-call(s32[16,2]{1,0:T(8,128)S(1)} %copy.24.incoming, bf16[2,128,256]{2,1,0:T(8,128)(2,1)S(1)} %copy-done, bf16[2,128,256]{2,1,0:T(8,128)(2,1)S(1)} %collective-permute-done.1.refs_1_, bf16[2,128,256]{2,1,0:T(8,128)(2,1)S(1)} %collective-permute-done.refs_2_, ...), custom_call_target="tpu_custom_call" | custom-call | bytes 4194304 | tf_op jit(solution)/shard_map/pick_blocks/pallas_call | solution.py:163
  28.7 3.7 %all-to-all-start.1 = ((bf16[32,128,256]{2,1,0:T(8,128)(2,1)}), bf16[32,128,256]{2,1,0:T(8,128)(2,1)S(1)}, u32[]{:S(2)}, u32[]{:S(2)}) async-start(bf16[32,128,256]{2,1,0:T(8,128)(2,1)} %pick_blocks.1), calls=%async_computation.1 | async-start | bytes 4194304 | tf_op jit(solution)/shard_map/all_to_all | solution.py:393
  32.5 0.0 copy-start.1
  32.5 0.0 copy-start.2
  32.5 16.3 %densify.3.dense = bf16[2048,4096]{1,0:T(8,128)(2,1)} custom-call(s32[512]{0:T(512)S(1)} %get-tuple-element.42.target, s32[512]{0:T(512)S(1)} %select_reduce_fusion.1.members, s32[513]{0:T(1024)S(1)} %convert_reduce_fusion.starts, s32[256]{0:T(256)S(1)} %select_reduce_fusion.2.shared, s32[17]{0:T(128)S(1)} %slice.33.ends, ...), custom_call_target="tpu_custom_call", output_to_operand_aliasing={{}: (6, {})} | custom-call | bytes 33554432 | tf_op jit(solution)/shard_map/densify/pallas_call | solution.py:111
  48.8 4.7 %all-to-all-done.1 = bf16[32,128,256]{2,1,0:T(8,128)(2,1)S(1)} async-done(((bf16[32,128,256]{2,1,0:T(8,128)(2,1)}), bf16[32,128,256]{2,1,0:T(8,128)(2,1)S(1)}, u32[]{:S(2)}, u32[]{:S(2)}) %all-to-all-start.1) | async-done | bytes 2097184 | tf_op jit(solution)/shard_map/all_to_all | solution.py:393
  53.5 15.6 %layer.1 = (bf16[2048,256]{1,0:T(8,128)(2,1)}, bf16[16,544,128]{2,1,0:T(8,128)(2,1)S(1)}) custom-call(bf16[2048,4096]{1,0:T(8,128)(2,1)} %densify.3.dense, bf16[4096,256]{1,0:T(8,128)(2,1)S(1)} %bitcast.16, bf16[256,256]{1,0:T(8,128)(2,1)S(1)} %copy-done.2, bf16[2048,256]{1,0:T(8,128)(2,1)S(1)} %copy-done.1), custom_call_target="tpu_custom_call" | custom-call | flops 8589934592 | bytes 16777216 | tf_op jit(solution)/shard_map/layer/pallas_call | solution.py:266
  69.2 22.3 %all_to_all.27.returned = bf16[16,544,128]{2,1,0:T(8,128)(2,1)S(1)} all-to-all(bf16[16,544,128]{2,1,0:T(8,128)(2,1)S(1)} %get-tuple-element.26), channel_id=1, replica_groups=mesh['row'=8,'col'=16] {'col'}, dimensions={0} | all-to-all | bytes 4456448 | tf_op jit(solution)/shard_map/all_to_all | solution.py:393
  91.5 1.9 %group_sums.1 = (f32[8,256,128]{2,1,0:T(8,128)S(1)}, bf16[8,256,128]{2,1,0:T(8,128)(2,1)S(1)}) custom-call(s32[16,2]{1,0:T(8,128)S(1)} %copy.24.incoming, bf16[16,544,128]{2,1,0:T(8,128)(2,1)S(1)} %all_to_all.27.returned), custom_call_target="tpu_custom_call" | custom-call | flops 1114112 | bytes 4456448 | tf_op jit(solution)/shard_map/group_sums/pallas_call | solution.py:315
  93.4 13.1 %collective-permute-start.7 = (bf16[8,256,128]{2,1,0:T(8,128)(2,1)S(1)}, bf16[8,256,128]{2,1,0:T(8,128)(2,1)S(1)}, u32[]{:S(2)}, u32[]{:S(2)}) collective-permute-start(bf16[8,256,128]{2,1,0:T(8,128)(2,1)S(1)} %get-tuple-element.28), channel_id=1, source_target_pairs={{0,16},{16,0},{32,48},{48,32},{64,80},{80,64},{96,112},{112,96},{1... | collective-permute-start | bytes 1572872 | tf_op jit(solution)/shard_map/ppermute | solution.py:396
  106.5 0.1 collective-permute-start.8
  106.6 1.4 %collective-permute-done.8 = f32[32,128]{1,0:T(8,128)S(1)} collective-permute-done((f32[32,128]{1,0:T(8,128)S(1)}, f32[32,128]{1,0:T(8,128)S(1)}, u32[]{:S(2)}, u32[]{:S(2)}) %collective-permute-start.8) | collective-permute-done | bytes 16416 | tf_op jit(solution)/shard_map/ppermute | solution.py:396
  108.1 1.1 collective-permute-start.11
  109.1 1.0 collective-permute-start.10
  110.1 1.8 %collective-permute-start.9 = (f32[32,128]{1,0:T(8,128)S(1)}, f32[32,128]{1,0:T(8,128)S(1)}, u32[]{:S(2)}, u32[]{:S(2)}) collective-permute-start(f32[32,128]{1,0:T(8,128)S(1)} %add.41), channel_id=1, source_target_pairs={{0,64},{16,80},{32,96},{48,112},{64,0},{80,16},{96,32},{112,48},{1... | collective-permute-start | bytes 49160 | tf_op jit(solution)/shard_map/ppermute | solution.py:399
  112.0 0.0 collective-permute-done.11
  112.0 2.1 %collective-permute-done.10 = f32[32,128]{1,0:T(8,128)S(1)} collective-permute-done((f32[32,128]{1,0:T(8,128)S(1)}, f32[32,128]{1,0:T(8,128)S(1)}, u32[]{:S(2)}, u32[]{:S(2)}) %collective-permute-start.10) | collective-permute-done | bytes 16416 | tf_op jit(solution)/shard_map/ppermute | solution.py:399
  114.1 1.3 collective-permute-done.9
  115.4 0.0 collective-permute-done.7.arrived
  115.4 0.1 chip_sums.1
  115.5 0.7 broadcast_in_dim.75
  116.2 3.5 %all-to-all-start.3 = ((bf16[16,32,128]{2,1,0:T(8,128)(2,1)}), bf16[16,32,128]{2,1,0:T(8,128)(2,1)S(1)}, u32[]{:S(2)}, u32[]{:S(2)}) async-start(bf16[16,32,128]{2,1,0:T(8,128)(2,1)} %broadcast_in_dim.75), calls=%async_computation.3 | async-start | bytes 262144 | tf_op jit(solution)/shard_map/all_to_all | solution.py:393
  119.7 1.9 %collective-permute-start.12 = (bf16[2,256,128]{2,1,0:T(8,128)(2,1)S(1)}, bf16[2,256,128]{2,1,0:T(8,128)(2,1)S(1)}, u32[]{:S(2)}, u32[]{:S(2)}) collective-permute-start(bf16[2,256,128]{2,1,0:T(8,128)(2,1)S(1)} %get-tuple-element.36), channel_id=1, source_target_pairs={{0,32},{16,48},{32,64},{48,80},{64,96},{80,112},{96,0},{112,16},{1... | collective-permute-start | bytes 393224 | tf_op jit(solution)/shard_map/ppermute | solution.py:399
  121.6 1.9 %collective-permute-start.13 = (bf16[2,256,128]{2,1,0:T(8,128)(2,1)S(1)}, bf16[2,256,128]{2,1,0:T(8,128)(2,1)S(1)}, u32[]{:S(2)}, u32[]{:S(2)}) collective-permute-start(bf16[2,256,128]{2,1,0:T(8,128)(2,1)S(1)} %get-tuple-element.37), channel_id=1, source_target_pairs={{0,64},{16,80},{32,96},{48,112},{64,0},{80,16},{96,32},{112,48},{1... | collective-permute-start | bytes 393224 | tf_op jit(solution)/shard_map/ppermute | solution.py:399
  123.5 0.9 collective-permute-start.14
  124.3 3.3 %all-to-all-done.3 = bf16[16,32,128]{2,1,0:T(8,128)(2,1)S(1)} async-done(((bf16[16,32,128]{2,1,0:T(8,128)(2,1)}), bf16[16,32,128]{2,1,0:T(8,128)(2,1)S(1)}, u32[]{:S(2)}, u32[]{:S(2)}) %all-to-all-start.3) | async-done | bytes 131104 | tf_op jit(solution)/shard_map/all_to_all | solution.py:393
  127.7 0.1 copy.26
  127.8 0.7 copy.29
  128.5 0.0 collective-permute-done.12.refs_0_
  128.5 0.0 collective-permute-done.13.refs_1_
  128.5 0.0 collective-permute-done.14.refs_2_
  128.5 0.8 owner_sum.1
  (9 shorter events, 0.1 us)
Async XLA Ops:
  0.6 22.2 %collective-permute-start.2 = (bf16[2,128,256]{2,1,0:T(8,128)(2,1)}, bf16[2,128,256]{2,1,0:T(8,128)(2,1)S(1)}, u32[]{:S(2)}, u32[]{:S(2)}) collective-permute-start(bf16[2,128,256]{2,1,0:T(8,128)(2,1)} %refs_0_.1), channel_id=1, source_target_pairs={{0,96},{16,112},{32,0},{48,16},{64,32},{80,48},{96,64},{112,80},{1... | collective-permute-start | bytes 393224 | tf_op jit(solution)/shard_map/ppermute | solution.py:399
  3.5 19.8 %collective-permute-start.1 = (bf16[2,128,256]{2,1,0:T(8,128)(2,1)}, bf16[2,128,256]{2,1,0:T(8,128)(2,1)S(1)}, u32[]{:S(2)}, u32[]{:S(2)}) collective-permute-start(bf16[2,128,256]{2,1,0:T(8,128)(2,1)} %refs_0_.1), channel_id=1, source_target_pairs={{0,32},{16,48},{32,64},{48,80},{64,96},{80,112},{96,0},{112,16},{1... | collective-permute-start | bytes 393224 | tf_op jit(solution)/shard_map/ppermute | solution.py:399
  3.5 19.3 %collective-permute-start = (bf16[2,128,256]{2,1,0:T(8,128)(2,1)}, bf16[2,128,256]{2,1,0:T(8,128)(2,1)S(1)}, u32[]{:S(2)}, u32[]{:S(2)}) collective-permute-start(bf16[2,128,256]{2,1,0:T(8,128)(2,1)} %refs_0_.1), channel_id=1, source_target_pairs={{0,64},{16,80},{32,96},{48,112},{64,0},{80,16},{96,32},{112,48},{1... | collective-permute-start | bytes 393224 | tf_op jit(solution)/shard_map/ppermute | solution.py:399
  5.8 19.1 %collective-permute-start.3 = (bf16[2,128,256]{2,1,0:T(8,128)(2,1)}, bf16[2,128,256]{2,1,0:T(8,128)(2,1)S(1)}, u32[]{:S(2)}, u32[]{:S(2)}) collective-permute-start(bf16[2,128,256]{2,1,0:T(8,128)(2,1)} %refs_0_.1), channel_id=1, source_target_pairs={{0,16},{16,0},{32,48},{48,32},{64,80},{80,64},{96,112},{112,96},{1... | collective-permute-start | bytes 393224 | tf_op jit(solution)/shard_map/ppermute | solution.py:396
  7.2 15.5 %all-to-all-start = ((s32[16,1,2]{2,1,0:T(1,128)}), s32[16,1,2]{2,1,0:T(1,128)S(1)}, u32[]{:S(2)}, u32[]{:S(2)}) async-start(s32[16,1,2]{2,1,0:T(1,128)} %copy.22), calls=%async_computation | async-start | bytes 16384 | tf_op jit(solution)/shard_map/all_to_all | solution.py:393
  22.8 2.1 %collective-permute-start.5 = (bf16[2,128,256]{2,1,0:T(8,128)(2,1)S(1)}, bf16[2,128,256]{2,1,0:T(8,128)(2,1)S(1)}, u32[]{:S(2)}, u32[]{:S(2)}) collective-permute-start(bf16[2,128,256]{2,1,0:T(8,128)(2,1)S(1)} %collective-permute-done.refs_2_), channel_id=1, source_target_pairs={{0,16},{16,0},{32,48},{48,32},{64,80},{80,64},{96,112},{112,96},{1... | collective-permute-start | bytes 393224 | tf_op jit(solution)/shard_map/ppermute | solution.py:396
  22.8 2.1 %collective-permute-start.6 = (bf16[2,128,256]{2,1,0:T(8,128)(2,1)S(1)}, bf16[2,128,256]{2,1,0:T(8,128)(2,1)S(1)}, u32[]{:S(2)}, u32[]{:S(2)}) collective-permute-start(bf16[2,128,256]{2,1,0:T(8,128)(2,1)S(1)} %collective-permute-done.2.refs_3_), channel_id=1, source_target_pairs={{0,16},{16,0},{32,48},{48,32},{64,80},{80,64},{96,112},{112,96},{1... | collective-permute-start | bytes 393224 | tf_op jit(solution)/shard_map/ppermute | solution.py:396
  23.3 1.6 %collective-permute-start.4 = (bf16[2,128,256]{2,1,0:T(8,128)(2,1)S(1)}, bf16[2,128,256]{2,1,0:T(8,128)(2,1)S(1)}, u32[]{:S(2)}, u32[]{:S(2)}) collective-permute-start(bf16[2,128,256]{2,1,0:T(8,128)(2,1)S(1)} %collective-permute-done.1.refs_1_), channel_id=1, source_target_pairs={{0,16},{16,0},{32,48},{48,32},{64,80},{80,64},{96,112},{112,96},{1... | collective-permute-start | bytes 393224 | tf_op jit(solution)/shard_map/ppermute | solution.py:396
  23.9 1.1 copy-start
  28.7 24.8 %all-to-all-start.1 = ((bf16[32,128,256]{2,1,0:T(8,128)(2,1)}), bf16[32,128,256]{2,1,0:T(8,128)(2,1)S(1)}, u32[]{:S(2)}, u32[]{:S(2)}) async-start(bf16[32,128,256]{2,1,0:T(8,128)(2,1)} %pick_blocks.1), calls=%async_computation.1 | async-start | bytes 4194304 | tf_op jit(solution)/shard_map/all_to_all | solution.py:393
  32.5 21.0 %copy-start.1 = (bf16[2048,256]{1,0:T(8,128)(2,1)S(1)}, bf16[2048,256]{1,0:T(8,128)(2,1)}, u32[]{:S(2)}) copy-start(bf16[2048,256]{1,0:T(8,128)(2,1)} %cotangent.1) | copy-start | bytes 3145732
  32.5 21.0 %copy-start.2 = (bf16[256,256]{1,0:T(8,128)(2,1)S(1)}, bf16[256,256]{1,0:T(8,128)(2,1)}, u32[]{:S(2)}) copy-start(bf16[256,256]{1,0:T(8,128)(2,1)} %weight.1) | copy-start | bytes 393220
  93.4 22.0 %collective-permute-start.7 = (bf16[8,256,128]{2,1,0:T(8,128)(2,1)S(1)}, bf16[8,256,128]{2,1,0:T(8,128)(2,1)S(1)}, u32[]{:S(2)}, u32[]{:S(2)}) collective-permute-start(bf16[8,256,128]{2,1,0:T(8,128)(2,1)S(1)} %get-tuple-element.28), channel_id=1, source_target_pairs={{0,16},{16,0},{32,48},{48,32},{64,80},{80,64},{96,112},{112,96},{1... | collective-permute-start | bytes 1572872 | tf_op jit(solution)/shard_map/ppermute | solution.py:396
  106.5 1.5 %collective-permute-start.8 = (f32[32,128]{1,0:T(8,128)S(1)}, f32[32,128]{1,0:T(8,128)S(1)}, u32[]{:S(2)}, u32[]{:S(2)}) collective-permute-start(f32[32,128]{1,0:T(8,128)S(1)} %convert_reduce_fusion.2), channel_id=1, source_target_pairs={{0,16},{16,0},{32,48},{48,32},{64,80},{80,64},{96,112},{112,96},{1... | collective-permute-start | bytes 49160 | tf_op jit(solution)/shard_map/ppermute | solution.py:396
  108.1 3.9 %collective-permute-start.11 = (f32[32,128]{1,0:T(8,128)S(1)}, f32[32,128]{1,0:T(8,128)S(1)}, u32[]{:S(2)}, u32[]{:S(2)}) collective-permute-start(f32[32,128]{1,0:T(8,128)S(1)} %add.41), channel_id=1, source_target_pairs={{0,96},{16,112},{32,0},{48,16},{64,32},{80,48},{96,64},{112,80},{1... | collective-permute-start | bytes 49160 | tf_op jit(solution)/shard_map/ppermute | solution.py:399
  109.1 4.9 %collective-permute-start.10 = (f32[32,128]{1,0:T(8,128)S(1)}, f32[32,128]{1,0:T(8,128)S(1)}, u32[]{:S(2)}, u32[]{:S(2)}) collective-permute-start(f32[32,128]{1,0:T(8,128)S(1)} %add.41), channel_id=1, source_target_pairs={{0,32},{16,48},{32,64},{48,80},{64,96},{80,112},{96,0},{112,16},{1... | collective-permute-start | bytes 49160 | tf_op jit(solution)/shard_map/ppermute | solution.py:399
  110.1 5.2 %collective-permute-start.9 = (f32[32,128]{1,0:T(8,128)S(1)}, f32[32,128]{1,0:T(8,128)S(1)}, u32[]{:S(2)}, u32[]{:S(2)}) collective-permute-start(f32[32,128]{1,0:T(8,128)S(1)} %add.41), channel_id=1, source_target_pairs={{0,64},{16,80},{32,96},{48,112},{64,0},{80,16},{96,32},{112,48},{1... | collective-permute-start | bytes 49160 | tf_op jit(solution)/shard_map/ppermute | solution.py:399
  116.2 11.5 %all-to-all-start.3 = ((bf16[16,32,128]{2,1,0:T(8,128)(2,1)}), bf16[16,32,128]{2,1,0:T(8,128)(2,1)S(1)}, u32[]{:S(2)}, u32[]{:S(2)}) async-start(bf16[16,32,128]{2,1,0:T(8,128)(2,1)} %broadcast_in_dim.75), calls=%async_computation.3 | async-start | bytes 262144 | tf_op jit(solution)/shard_map/all_to_all | solution.py:393
  119.7 8.8 %collective-permute-start.12 = (bf16[2,256,128]{2,1,0:T(8,128)(2,1)S(1)}, bf16[2,256,128]{2,1,0:T(8,128)(2,1)S(1)}, u32[]{:S(2)}, u32[]{:S(2)}) collective-permute-start(bf16[2,256,128]{2,1,0:T(8,128)(2,1)S(1)} %get-tuple-element.36), channel_id=1, source_target_pairs={{0,32},{16,48},{32,64},{48,80},{64,96},{80,112},{96,0},{112,16},{1... | collective-permute-start | bytes 393224 | tf_op jit(solution)/shard_map/ppermute | solution.py:399
  121.6 7.0 %collective-permute-start.13 = (bf16[2,256,128]{2,1,0:T(8,128)(2,1)S(1)}, bf16[2,256,128]{2,1,0:T(8,128)(2,1)S(1)}, u32[]{:S(2)}, u32[]{:S(2)}) collective-permute-start(bf16[2,256,128]{2,1,0:T(8,128)(2,1)S(1)} %get-tuple-element.37), channel_id=1, source_target_pairs={{0,64},{16,80},{32,96},{48,112},{64,0},{80,16},{96,32},{112,48},{1... | collective-permute-start | bytes 393224 | tf_op jit(solution)/shard_map/ppermute | solution.py:399
  123.5 5.1 %collective-permute-start.14 = (bf16[2,256,128]{2,1,0:T(8,128)(2,1)S(1)}, bf16[2,256,128]{2,1,0:T(8,128)(2,1)S(1)}, u32[]{:S(2)}, u32[]{:S(2)}) collective-permute-start(bf16[2,256,128]{2,1,0:T(8,128)(2,1)S(1)} %get-tuple-element.38), channel_id=1, source_target_pairs={{0,96},{16,112},{32,0},{48,16},{64,32},{80,48},{96,64},{112,80},{1... | collective-permute-start | bytes 393224 | tf_op jit(solution)/shard_map/ppermute | solution.py:399
